TPU v7x, 32 devices: a whole 2x2x4 slice. The times are simulated.
32 devices in a mesh: seq: 8 (over z, x), freq: 4 (over y, core).
Axes of the slice: x: 2, y: 2, z: 4, core: 2. Of those that a mesh axis runs over, the one named last changes fastest.
Arguments:
- tokens: bfloat16 [8, 3072, 768], P('seq', 'freq'), may hold values from -6 to 6
- freq_ids: int32 [8, 3072], P('seq', 'freq'), may hold values from 0 to 11, as said below
- clip_ids: int32 [8, 3072], P('seq'), may hold values from 0 to 7, as said below
- cotangent: bfloat16 [8, 3072, 768], P('seq', 'freq'), may hold values from -6 to 6
- ln1_gain: bfloat16 [768], P(('seq', 'freq')), may hold values from 0.25 to 1.75
- first_norm_bias: bfloat16 [768], P(('seq', 'freq')), may hold values from -1.75 to 1.75
- qkv_weight: bfloat16 [768, 2304], P(('seq', 'freq')), may hold values from -0.3125 to 0.3125
- q_bias: bfloat16 [768], P(('seq', 'freq')), may hold values from -3 to 3
- v_bias: bfloat16 [768], P(('seq', 'freq')), may hold values from -3 to 3
- out_weight: bfloat16 [768, 768], P(('seq', 'freq')), may hold values from -0.875 to 0.875
- out_bias: bfloat16 [768], P(('seq', 'freq')), may hold values from -1.75 to 1.75
- ln2_gain: bfloat16 [768], P(('seq', 'freq')), may hold values from 0.25 to 1.75
- ln2_bias: bfloat16 [768], P(('seq', 'freq')), may hold values from -1.75 to 1.75
- up_weight: bfloat16 [768, 3072], P(('seq', 'freq')), may hold values from -0.21875 to 0.21875
- up_bias: bfloat16 [3072], P(('seq', 'freq')), may hold values from -3 to 3
- down_weight: bfloat16 [3072, 768], P(('seq', 'freq')), may hold values from -0.21875 to 0.21875
- down_bias: bfloat16 [768], P(('seq', 'freq')), may hold values from -1.75 to 1.75
- freq_table: bfloat16 [768, 12], P(('seq', 'freq')), may hold values from -3 to 3
Outputs:
- mixed: bfloat16 [8, 3072, 768], P('seq', 'freq')
- input_grad: bfloat16 [8, 3072, 768], P('seq', 'freq')
- grad_ln1_gain: float32 [768], P(('seq', 'freq'))
- grad_ln1_bias: float32 [768], P(('seq', 'freq'))
- grad_qkv_weight: float32 [768, 2304], P(('seq', 'freq'))
- grad_q_bias: float32 [768], P(('seq', 'freq'))
- grad_v_bias: float32 [768], P(('seq', 'freq'))
- grad_out_weight: float32 [768, 768], P(('seq', 'freq'))
- grad_out_bias: float32 [768], P(('seq', 'freq'))
- grad_ln2_gain: float32 [768], P(('seq', 'freq'))
- grad_ln2_bias: float32 [768], P(('seq', 'freq'))
- grad_up_weight: float32 [768, 3072], P(('seq', 'freq'))
- grad_up_bias: float32 [3072], P(('seq', 'freq'))
- grad_down_weight: float32 [3072, 768], P(('seq', 'freq'))
- grad_down_bias: float32 [768], P(('seq', 'freq'))
- grad_freq_table: float32 [768, 12], P(('seq', 'freq'))
Inputs may be any that keep to these rules, and one draw needn't show every extreme that they name: `clip_ids`: within each of the 4 aligned groups of 768 positions of a sequence, clip ids never fall and every clip 0 to 7 occurs. `freq_ids`: positions in the k-th aligned group of 768 positions of a sequence have frequency rows k * (3) to (k + 1) * 3 - 1.
All inputs are finite; a program needn't handle non-finite values.
Results may differ from a plain program's by a relative error of at most 0.015.
Values may be sent and summed in bfloat16 or wider, within the bound.
No kernel may reach another device: no remote copies, remote signals or barrier semaphores. Data moves between devices by JAX's collectives and lax.ppermute only.
A program may use at most 512 MiB of HBM per device.

v0:
```python
import math

import jax
import jax.numpy as jnp
from jax import lax
from jax.sharding import PartitionSpec as P

HEADS = 12
HEAD_DIM = 64
FREQS = 12


epsilon = 1e-06
masked_score = -1e30


def layer_norm(values, gain_vec, shift_vec):
    center = values - jnp.mean(values, axis=-1, keepdims=True)
    spread = jnp.mean(center * center, axis=-1, keepdims=True)
    return center * lax.rsqrt(spread + epsilon) * gain_vec + shift_vec


def exact_gelu(values):
    return jax.nn.gelu(values, approximate=False)


def local(
    tokens,
    freq_ids,
    clip_ids,
    cotangent,
    ln1_gain,
    first_norm_bias,
    qkv_weight,
    q_bias,
    v_bias,
    out_weight,
    out_bias,
    ln2_gain,
    ln2_bias,
    up_weight,
    up_bias,
    down_weight,
    down_bias,
    freq_table,
):
    wide = jnp.float32
    narrow = jnp.bfloat16
    gathered = (
        lax.all_gather(ln1_gain, ("seq", "freq"), axis=0, tiled=True),
        lax.all_gather(first_norm_bias, ("seq", "freq"), axis=0, tiled=True),
        lax.all_gather(qkv_weight, ("seq", "freq"), axis=0, tiled=True),
        lax.all_gather(q_bias, ("seq", "freq"), axis=0, tiled=True),
        lax.all_gather(v_bias, ("seq", "freq"), axis=0, tiled=True),
        lax.all_gather(out_weight, ("seq", "freq"), axis=0, tiled=True),
        lax.all_gather(out_bias, ("seq", "freq"), axis=0, tiled=True),
        lax.all_gather(ln2_gain, ("seq", "freq"), axis=0, tiled=True),
        lax.all_gather(ln2_bias, ("seq", "freq"), axis=0, tiled=True),
        lax.all_gather(up_weight, ("seq", "freq"), axis=0, tiled=True),
        lax.all_gather(up_bias, ("seq", "freq"), axis=0, tiled=True),
        lax.all_gather(down_weight, ("seq", "freq"), axis=0, tiled=True),
        lax.all_gather(down_bias, ("seq", "freq"), axis=0, tiled=True),
        lax.all_gather(freq_table, ("seq", "freq"), axis=0, tiled=True),
    )
    (
        full_ln1_gain,
        full_ln1_bias,
        full_qkv,
        full_q_bias,
        full_v_bias,
        full_out,
        full_out_bias,
        full_ln2_gain,
        full_ln2_bias,
        full_up,
        full_up_bias,
        full_down,
        full_down_bias,
        full_table,
    ) = gathered
    seq_dev, group_len, feature = tokens.shape
    whole_len = clip_ids.shape[1]
    head_count = HEADS
    head_size = HEAD_DIM
    per_block = 2
    block_count = head_count // per_block
    score_scale = 1.0 / math.sqrt(head_size)
    patches = seq_dev * group_len
    freq_place = lax.axis_index("freq")
    own_clips = lax.dynamic_slice_in_dim(clip_ids, freq_place * group_len, group_len, 1)
    same_clip = (own_clips[:, :, None] == clip_ids[:, None, :])[:, None]
    onehot = (freq_ids.reshape(patches, 1) == jnp.arange(FREQS, dtype=jnp.int32)[None, :]).astype(
        wide
    )
    inputs_wide = tokens.reshape(patches, feature).astype(wide)
    hidden = inputs_wide + jnp.dot(
        onehot, full_table.astype(wide).T, precision=lax.Precision.HIGHEST
    )
    normed, first_pull = jax.vjp(
        layer_norm, hidden, full_ln1_gain.astype(wide), full_ln1_bias.astype(wide)
    )
    normed_low = normed.astype(narrow)
    projected = jnp.dot(normed_low, full_qkv, preferred_element_type=wide)
    queries_flat = (projected[:, :feature] + full_q_bias.astype(wide)).astype(narrow)
    queries_flat = queries_flat.reshape(seq_dev, group_len, feature)
    queries = queries_flat.reshape(seq_dev, group_len, head_count, head_size)
    keys_local = (
        projected[:, feature : 2 * feature].astype(narrow).reshape(seq_dev, group_len, feature)
    )
    values_local = (projected[:, 2 * feature :] + full_v_bias.astype(wide)).astype(narrow)
    values_local = values_local.reshape(seq_dev, group_len, feature)
    all_keys, all_values = (
        lax.all_gather(keys_local, "freq", axis=1, tiled=True),
        lax.all_gather(values_local, "freq", axis=1, tiled=True),
    )
    all_keys = all_keys.reshape(seq_dev, whole_len, head_count, head_size)
    all_values = all_values.reshape(seq_dev, whole_len, head_count, head_size)

    def block_scores(first_head):
        unscaled_scores = jnp.einsum(
            "sqhe,skhe->shqk",
            queries[:, :, first_head : first_head + per_block],
            all_keys[:, :, first_head : first_head + per_block],
            preferred_element_type=wide,
        )
        return jnp.where(same_clip, unscaled_scores * score_scale, masked_score)

    contexts = []
    log_totals = []
    for block_id in range(block_count):
        first_head = block_id * per_block
        scores = block_scores(first_head)
        row_max = jnp.max(scores, axis=-1, keepdims=True)
        row_total = jnp.sum(jnp.exp(scores - row_max), axis=-1, keepdims=True)
        log_total = row_max + jnp.log(row_total)
        attention_probability_map = jnp.exp(scores - log_total)
        contexts.append(
            jnp.einsum(
                "shqk,skhe->sqhe",
                attention_probability_map.astype(narrow),
                all_values[:, :, first_head : first_head + per_block],
                preferred_element_type=wide,
            )
        )
        log_totals.append(log_total)
    context_low = jnp.concatenate(contexts, axis=2).reshape(patches, feature).astype(narrow)
    middle = (
        hidden
        + jnp.dot(context_low, full_out, preferred_element_type=wide)
        + full_out_bias.astype(wide)
    )
    second, second_pull = jax.vjp(
        layer_norm, middle, full_ln2_gain.astype(wide), full_ln2_bias.astype(wide)
    )
    second_low = second.astype(narrow)
    upward = jnp.dot(second_low, full_up, preferred_element_type=wide) + full_up_bias.astype(wide)
    activated, gelu_pull = jax.vjp(exact_gelu, upward)
    activated_low = activated.astype(narrow)
    output = (
        middle
        + jnp.dot(activated_low, full_down, preferred_element_type=wide)
        + full_down_bias.astype(wide)
    )
    mixed = output.astype(narrow).reshape(seq_dev, group_len, feature)
    upstream = cotangent.reshape(patches, feature)
    upstream_wide = upstream.astype(wide)
    grad_down_bias = jnp.sum(upstream_wide, axis=0)
    grad_down_weight = jnp.einsum("ri,rj->ij", activated_low, upstream, preferred_element_type=wide)
    grad_activated = jnp.einsum("rj,ij->ri", upstream, full_down, preferred_element_type=wide)
    grad_upward = gelu_pull(grad_activated)[0].astype(narrow)
    grad_up_bias = jnp.sum(grad_upward.astype(wide), axis=0)
    grad_up_weight = jnp.einsum("ri,rj->ij", second_low, grad_upward, preferred_element_type=wide)
    grad_second = jnp.einsum("rj,ij->ri", grad_upward, full_up, preferred_element_type=wide)
    grad_mid_norm, grad_ln2_gain, grad_ln2_bias = second_pull(grad_second)
    grad_middle = upstream_wide + grad_mid_norm
    grad_out_bias = jnp.sum(grad_middle, axis=0)
    grad_branch = grad_middle.astype(narrow)
    grad_out_weight = jnp.einsum("ri,rj->ij", context_low, grad_branch, preferred_element_type=wide)
    grad_context_flat = jnp.einsum(
        "rj,ij->ri", grad_branch, full_out, preferred_element_type=wide
    ).astype(narrow)
    grad_context_flat = grad_context_flat.reshape(seq_dev, group_len, feature)
    grad_context = grad_context_flat.reshape(seq_dev, group_len, head_count, head_size)
    query_grads = []
    key_grads = []
    value_grads = []
    for block_id in range(block_count):
        first_head = block_id * per_block
        scores = block_scores(first_head)
        attention_probability_map = jnp.exp(scores - log_totals[block_id])
        context_piece = grad_context[:, :, first_head : first_head + per_block]
        grad_prob = jnp.einsum(
            "sqhe,skhe->shqk",
            context_piece,
            all_values[:, :, first_head : first_head + per_block],
            preferred_element_type=wide,
        )
        inner_sum = jnp.sum(attention_probability_map * grad_prob, axis=-1, keepdims=True)
        grad_scores = (attention_probability_map * (grad_prob - inner_sum)).astype(narrow)
        query_grads.append(
            jnp.einsum(
                "shqk,skhe->sqhe",
                grad_scores,
                all_keys[:, :, first_head : first_head + per_block],
                preferred_element_type=wide,
            )
            * score_scale
        )
        key_grads.append(
            jnp.einsum(
                "shqk,sqhe->skhe",
                grad_scores,
                queries[:, :, first_head : first_head + per_block],
                preferred_element_type=wide,
            )
            * score_scale
        )
        value_grads.append(
            jnp.einsum(
                "shqk,sqhe->skhe",
                attention_probability_map.astype(narrow),
                context_piece,
                preferred_element_type=wide,
            )
        )
    key_part = jnp.concatenate(key_grads, axis=2).reshape(seq_dev, whole_len, feature)
    value_part = jnp.concatenate(value_grads, axis=2).reshape(seq_dev, whole_len, feature)
    key_sum, value_sum = (
        lax.psum_scatter(
            key_part.astype(jnp.bfloat16), "freq", scatter_dimension=1, tiled=True
        ).astype(jnp.float32),
        lax.psum_scatter(
            value_part.astype(jnp.bfloat16), "freq", scatter_dimension=1, tiled=True
        ).astype(jnp.float32),
    )
    grad_keys = key_sum.reshape(patches, feature).astype(narrow)
    grad_values = value_sum.reshape(patches, feature).astype(narrow)
    grad_queries = jnp.concatenate(query_grads, axis=2).reshape(patches, feature).astype(narrow)
    grad_q_bias = jnp.sum(grad_queries.astype(wide), axis=0)
    grad_v_bias = jnp.sum(grad_values.astype(wide), axis=0)
    grad_projected = jnp.concatenate([grad_queries, grad_keys, grad_values], axis=1)
    grad_qkv_weight = jnp.einsum(
        "ri,rj->ij", normed_low, grad_projected, preferred_element_type=wide
    )
    grad_normed = jnp.einsum("rj,ij->ri", grad_projected, full_qkv, preferred_element_type=wide)
    grad_hid_norm, grad_ln1_gain, grad_ln1_bias = first_pull(grad_normed)
    grad_hidden = grad_middle + grad_hid_norm
    input_grad = grad_hidden.astype(narrow).reshape(seq_dev, group_len, feature)
    grad_freq_table = jnp.einsum("rd,rf->df", grad_hidden, onehot, precision=lax.Precision.HIGHEST)
    summed = (
        lax.psum_scatter(grad_ln1_gain, ("seq", "freq"), scatter_dimension=0, tiled=True),
        lax.psum_scatter(grad_ln1_bias, ("seq", "freq"), scatter_dimension=0, tiled=True),
        lax.psum_scatter(grad_qkv_weight, ("seq", "freq"), scatter_dimension=0, tiled=True),
        lax.psum_scatter(grad_q_bias, ("seq", "freq"), scatter_dimension=0, tiled=True),
        lax.psum_scatter(grad_v_bias, ("seq", "freq"), scatter_dimension=0, tiled=True),
        lax.psum_scatter(grad_out_weight, ("seq", "freq"), scatter_dimension=0, tiled=True),
        lax.psum_scatter(grad_out_bias, ("seq", "freq"), scatter_dimension=0, tiled=True),
        lax.psum_scatter(grad_ln2_gain, ("seq", "freq"), scatter_dimension=0, tiled=True),
        lax.psum_scatter(grad_ln2_bias, ("seq", "freq"), scatter_dimension=0, tiled=True),
        lax.psum_scatter(grad_up_weight, ("seq", "freq"), scatter_dimension=0, tiled=True),
        lax.psum_scatter(grad_up_bias, ("seq", "freq"), scatter_dimension=0, tiled=True),
        lax.psum_scatter(grad_down_weight, ("seq", "freq"), scatter_dimension=0, tiled=True),
        lax.psum_scatter(grad_down_bias, ("seq", "freq"), scatter_dimension=0, tiled=True),
        lax.psum_scatter(grad_freq_table, ("seq", "freq"), scatter_dimension=0, tiled=True),
    )
    return (
        mixed,
        input_grad,
        summed[0],
        summed[1],
        summed[2],
        summed[3],
        summed[4],
        summed[5],
        summed[6],
        summed[7],
        summed[8],
        summed[9],
        summed[10],
        summed[11],
        summed[12],
        summed[13],
    )


def solution(mesh):
    in_specs = (
        P("seq", "freq", None),
        P("seq", "freq"),
        P("seq", None),
        P("seq", "freq", None),
        P(("seq", "freq")),
        P(("seq", "freq")),
        P(("seq", "freq"), None),
        P(("seq", "freq")),
        P(("seq", "freq")),
        P(("seq", "freq"), None),
        P(("seq", "freq")),
        P(("seq", "freq")),
        P(("seq", "freq")),
        P(("seq", "freq"), None),
        P(("seq", "freq")),
        P(("seq", "freq"), None),
        P(("seq", "freq")),
        P(("seq", "freq"), None),
    )
    out_specs = (
        P("seq", "freq", None),
        P("seq", "freq", None),
        P(("seq", "freq")),
        P(("seq", "freq")),
        P(("seq", "freq"), None),
        P(("seq", "freq")),
        P(("seq", "freq")),
        P(("seq", "freq"), None),
        P(("seq", "freq")),
        P(("seq", "freq")),
        P(("seq", "freq")),
        P(("seq", "freq"), None),
        P(("seq", "freq")),
        P(("seq", "freq"), None),
        P(("seq", "freq")),
        P(("seq", "freq"), None),
    )
    return jax.shard_map(local, mesh=mesh, in_specs=in_specs, out_specs=out_specs, check_vma=False)
```

profile of v0, /device:TPU:0, one launch (start us, length us, event | category | flops | bytes accessed | tf_op | source)
XLA Modules:
  0.0 1416.3 jit_solution(16752259010057267554)
XLA Ops:
  15.5 42.7 %all-reduce.20 = (bf16[768]{0:T(1024)(128)(2,1)S(1)}, bf16[768]{0:T(1024)(128)(2,1)S(1)}, bf16[768]{0:T(1024)(128)(2,1)}, bf16[768]{0:T(1024)(128)(2,1)}, bf16[7...) all-reduce(bf16[768]{0:T(1024)(128)(2,1)S(1)} %dynamic-update-slice, ...), channel_id=1, replica_groups=mesh['seq'=8,'freq'=4] {'seq','freq'}, use_global_device_ids=true, to_apply=%add.1 | all-reduce | flops 9216 | bytes 36864
  58.3 41.2 %all-gather.2 = bf16[32,24,12]{1,2,0:T(8,128)(2,1)S(1)} all-gather(bf16[1,24,12]{1,2,0:T(8,128)(2,1)} %bitcast.398), channel_id=1, replica_groups=mesh['seq'=8,'freq'=4] {'seq','freq'}, dimensions={0}, use_global_device_ids=true | all-gather | bytes 19008 | tf_op jit(solution)/shard_map/all_gather | solution.py:63
  104.3 5.6 fusion.118
  114.1 4.4 fusion.48
  128.5 19.2 %all-gather.20.cloned.1.call-done = bf16[3072,768]{1,0:T(8,128)(2,1)} async-done(((bf16[768,768]{1,0:T(8,128)(2,1)}), bf16[3072,768]{1,0:T(8,128)(2,1)}) %all-gather.20.cloned.1.call-update) | async-done | bytes 4718608 | tf_op jit(solution)/shard_map/all_gather | solution.py:113
  147.7 6.6 copy.78
  154.4 9.6 fusion.93
  164.0 8.0 fusion.91
  172.0 7.9 fusion.89
  180.0 7.9 fusion.85
  187.9 16.7 %fusion.5 = (f32[2,768]{1,0:T(2,128)S(1)}, f32[2,768]{1,0:T(2,128)S(1)}, f32[2,768,3072]{2,1,0:T(8,128)}) fusion(pred[768,3072]{1,0:T(8,128)(4,1)S(1)} %broadcast_compare_fusion, f32[2,768,3072]{2,1,0:T(8,128)} %fusion.85, bf16[1,3072,12,64]{1,3,2,0:T(8,128)(2,1)S(1)} %bitcast.343, bf16[1,768,12,64]{1,3,2,0:T(8,128)(2,1)S(1)} %bitcast.355), kind=kOutput, calls=%fused_computation.35 | convolution fusion | flops 632288256 | bytes 41103360 | tf_op jit(solution)/shard_map/sqhe,skhe->shqk/dot_general | solution.py:120
  204.6 38.4 %exponential_reduce_fusion = (f32[2,768]{1,0:T(2,128)S(1)}, f32[2,768]{1,0:T(2,128)S(1)}, f32[2,768]{1,0:T(2,128)S(1)}, f32[2,768]{1,0:T(2,128)S(1)}, f32[2,768]...) fusion(f32[2,768,3072]{2,1,0:T(8,128)} %get-tuple-element.122, f32[2,768]{1,0:T(2,128)S(1)} %get-tuple-element.80, ...), kind=kOutput, calls=%fused_computation.13 | convolution fusion | flops 698342400 | bytes 116637696 | tf_op jit(solution)/shard_map/sqhe,skhe->shqk/dot_general | solution.py:120
  243.6 27.6 %exponential_reduce_fusion.1 = (f32[2,768]{1,0:T(2,128)S(1)}, f32[2,768]{1,0:T(2,128)S(1)}, f32[2,768]{1,0:T(2,128)S(1)}, f32[2,768]{1,0:T(2,128)S(1)}) fusion(f32[2,768,3072]{2,1,0:T(8,128)} %fusion.93, f32[2,768]{1,0:T(2,128)S(1)} %get-tuple-element.78, pred[768,3072]{1,0:T(8,128)(4,1)S(1)} %broadcast_compare_fusion, f32[2,768]{1,0:T(2,128)S(1)} %get-tuple-element.75, ...), kind=kLoop, calls=%fused_computation.16 | loop fusion | flops 75491328 | bytes 77905920 | tf_op jit(solution)/shard_map/reduce_sum | solution.py:134
  271.9 6.7 copy.76
  278.6 9.5 fusion.72
  288.1 10.0 fusion.74
  298.1 9.2 fusion.76
  307.3 9.2 fusion.78
  316.6 9.2 fusion.80
  325.9 9.1 fusion.82
  335.0 3.8 fusion.125
  340.6 30.1 %multiply_convert_fusion.6 = (bf16[768,3072]{1,0:T(8,128)(2,1)}, f32[768,3072]{1,0:T(8,128)}, f32[768,3072]{1,0:T(8,128)}) fusion(f32[3072]{0:T(1024)} %convert_element_type.210, bf16[768,3072]{1,0:T(8,128)(2,1)} %all-gather.14.cloned.1.call-done, f32[768,768]{0,1:T(8,128)} %copy-done.5, f32[768]{0:T(1024)} %convert_element_type.208, ...), kind=kOutput, calls=%fused_computation.46 | convolution fusion | flops 3782541312 | bytes 30695424 | tf_op jit(solution)/shard_map/dot_general | solution.py:156
  370.7 4.2 all-gather.16.cloned.1.call-done
  374.9 12.5 convert_reduce_fusion
  387.4 6.0 fusion.127
  393.4 3.0 copy.81
  406.3 10.5 fusion.25
  416.8 7.9 fusion.92
  424.7 7.9 fusion.90
  432.6 7.9 fusion.88
  440.5 10.0 fusion.86
  450.5 9.2 fusion.84
  459.8 6.6 fusion.27
  466.4 11.3 fusion.29
  477.8 11.6 fusion.31
  489.4 6.6 fusion.33
  496.1 10.4 fusion.35
  506.5 76.5 %multiply_reduce_fusion = (f32[2,768]{1,0:T(2,128)}, f32[2,768]{1,0:T(2,128)}, f32[2,768]{1,0:T(2,128)}, f32[2,768]{1,0:T(2,128)}, f32[2,768]{1,0:T(2,128)}, /*index=5*/f32[2,768]{1,0:T(2,128)}, f32[2,768,3072]{2,1,0:T(8,128)}) fusion(f32[2,768,3072]{2,1,0:T(8,128)} %get-tuple-element.122, f32[2,768]{1,0:T(2,128)} %get-tuple-element.134, ...), kind=kOutput, calls=%fused_computation.1 | convolution fusion | flops 745528320 | bytes 229908480 | tf_op jit(solution)/shard_map/sqhe,skhe->shqk/dot_general | solution.py:192
  583.0 61.9 %multiply_convert_fusion = (bf16[2,768,3072]{2,1,0:T(8,128)(2,1)}, bf16[2,768,3072]{2,1,0:T(8,128)(2,1)}, bf16[2,768,3072]{2,1,0:T(8,128)(2,1)}, bf16[2,768,3072]{2,1,0:T(8,128)(2,1)}) fusion(f32[2,768,3072]{2,1,0:T(8,128)} %get-tuple-element.127, f32[2,768,3072]{2,1,0:T(8,128)} %get-tuple-element.122, f32[2,768]{1,0:T(2,128)} %get-tuple-element.68, ...), kind=kLoop, calls=%fused_computation | loop fusion | flops 113246208 | bytes 191152128 | tf_op jit(solution)/shard_map/convert_element_type | solution.py:199
  644.9 5.6 fusion.47
  650.5 5.6 fusion.45
  661.8 27.8 %multiply_convert_fusion.1 = (bf16[2,768,3072]{2,1,0:T(8,128)(2,1)}, bf16[2,768,3072]{2,1,0:T(8,128)(2,1)}) fusion(f32[2,768,3072]{2,1,0:T(8,128)} %fusion.92, f32[2,768,3072]{2,1,0:T(8,128)S(1)} %bitcast.326, f32[2,768]{1,0:T(2,128)S(1)} %copy-done.56, f32[2,768]{1,0:T(2,128)S(1)} %copy-done.37, pred[768,3072]{1,0:T(8,128)(4,1)} %copy-done.2, ...), kind=kLoop, calls=%fused_computation.2 | loop fusion | flops 56623104 | bytes 96755712 | tf_op jit(solution)/shard_map/convert_element_type | solution.py:199
  689.6 6.6 fusion.41
  696.2 4.4 fusion.39
  703.4 7.0 fusion.64
  710.5 8.7 fusion.62
  719.2 3.0 fusion.60
  722.2 6.9 fusion.58
  729.2 3.0 fusion.56
  732.2 3.1 fusion.54
  736.2 13.9 reduce-scatter.8.cloned.1.call-done
  750.1 7.6 fusion.126
  757.8 3.2 copy.82
  761.1 3.1 multiply_reduce_fusion.7
  768.9 4.6 fusion.96
  773.5 10.7 fusion.119
  784.5 10.3 fusion.65
  795.5 7.7 fusion.50
  804.8 7.7 fusion.52
  818.2 77.3 %all-reduce.23.cloned.1.call-done = (f32[768]{0:T(1024)}, f32[768]{0:T(1024)}, f32[768]{0:T(1024)}, f32[768]{0:T(1024)}, f32[768]{0:T(1024)}, /*index=5*/f32[768...) async-done(((f32[768]{0:T(1024)}, f32[768]{0:T(1024)}, f32[768]{0:T(1024)}, f32[768]{0:T(1024)}, f32[768]{0:T(1024)}, /*index=5*/f32[768]{0:T(1024)}, ...) | async-done | bytes 73744
  908.2 93.8 %reduce-scatter.14.cloned.1.call-done = f32[24,768]{1,0:T(8,128)} async-done(((f32[768,768]{1,0:T(8,128)}), f32[24,768]{1,0:T(8,128)}) %reduce-scatter.14.cloned.1.call-update) | async-done | bytes 73744 | tf_op jit(solution)/shard_map/reduce_scatter | solution.py:256
  1002.0 141.1 %reduce-scatter.16.cloned.1.call-done = f32[24,3072]{1,0:T(8,128)} async-done(((f32[768,3072]{1,0:T(8,128)}), f32[24,3072]{1,0:T(8,128)}) %reduce-scatter.16.cloned.1.call-update) | async-done | bytes 294928 | tf_op jit(solution)/shard_map/reduce_scatter | solution.py:260
  1143.1 141.8 %reduce-scatter.18.cloned.1.call-done = f32[96,768]{1,0:T(8,128)} async-done(((f32[3072,768]{1,0:T(8,128)}), f32[96,768]{1,0:T(8,128)}) %reduce-scatter.18.cloned.1.call-update) | async-done | bytes 294928 | tf_op jit(solution)/shard_map/reduce_scatter | solution.py:262
  1284.9 124.6 %reduce-scatter.12.cloned.1.call-done = f32[24,2304]{1,0:T(8,128)} async-done(((f32[768,2304]{1,0:T(8,128)}), f32[24,2304]{1,0:T(8,128)}) %reduce-scatter.12.cloned.1.call-update) | async-done | bytes 221200 | tf_op jit(solution)/shard_map/reduce_scatter | solution.py:253
  (312 shorter events, 74.9 us)
Async XLA Ops:
  7.2 97.1 %all-gather.10.cloned.1.call-start = ((), (), s32[]{:S(2)}) async-start(), calls=%async_computation.6 | async-start | bytes 3649536 | tf_op jit(solution)/shard_map/all_gather | solution.py:52
  7.9 139.8 %all-gather.20.cloned.1.call-start = ((), (), s32[]{:S(2)}) async-start(), calls=%async_computation.17 | async-start | bytes 5898240 | tf_op jit(solution)/shard_map/all_gather | solution.py:113
  58.3 51.7 %copy-start.32 = (f32[768]{0:T(1024)}, f32[768]{0:T(1024)S(1)}, u32[]{:S(2)}) copy-start(f32[768]{0:T(1024)S(1)} %convert_element_type.193) | copy-start | bytes 9220
  58.3 51.7 %copy-start.28 = (f32[768]{0:T(1024)}, f32[768]{0:T(1024)S(1)}, u32[]{:S(2)}) copy-start(f32[768]{0:T(1024)S(1)} %convert_element_type.192) | copy-start | bytes 9220
  104.3 9.8 copy-start.64
  104.3 9.8 copy-start.63
  114.0 9.3 copy-start.22
  114.0 157.9 %all-gather.18.cloned.1.call-start = ((), (), s32[]{:S(2)}) async-start(), calls=%async_computation.16 | async-start | bytes 5898240 | tf_op jit(solution)/shard_map/all_gather | solution.py:114
  114.1 10.6 copy-start.57
  118.5 216.5 %all-gather.12.cloned.1.call-start = ((), (), s32[]{:S(2)}) async-start(), calls=%async_computation.7 | async-start | bytes 1216512 | tf_op jit(solution)/shard_map/all_gather | solution.py:55
  119.1 221.5 %all-gather.14.cloned.1.call-start = ((), (), s32[]{:S(2)}) async-start(), calls=%async_computation.8 | async-start | bytes 4866048 | tf_op jit(solution)/shard_map/all_gather | solution.py:59
  119.7 255.2 %all-gather.16.cloned.1.call-start = ((), (), s32[]{:S(2)}) async-start(), calls=%async_computation.9 | async-start | bytes 4866048 | tf_op jit(solution)/shard_map/all_gather | solution.py:61
  120.3 616.0 %reduce-scatter.10.cloned.1.call-start = ((), (), s32[]{:S(2)}) async-start(), calls=%async_computation.11 | async-start | bytes 5898240 | tf_op jit(solution)/shard_map/reduce_scatter | solution.py:232
  126.1 456.9 %copy-start.2 = (pred[768,3072]{1,0:T(8,128)(4,1)}, pred[768,3072]{1,0:T(8,128)(4,1)S(1)}, u32[]{:S(2)}) copy-start(pred[768,3072]{1,0:T(8,128)(4,1)S(1)} %broadcast_compare_fusion) | copy-start | bytes 7077892
  128.5 76.1 %copy-start.12 = (bf16[768,768]{0,1:T(8,128)(2,1)}, bf16[768,768]{0,1:T(8,128)(2,1)S(1)}, u32[]{:S(2)}) copy-start(bf16[768,768]{0,1:T(8,128)(2,1)S(1)} %copy.77) | copy-start | bytes 3538948
  154.4 9.7 copy-start.11
  271.3 36.1 %copy-start.38 = (f32[2,768]{1,0:T(2,128)}, f32[2,768]{1,0:T(2,128)S(1)}, u32[]{:S(2)}) copy-start(f32[2,768]{1,0:T(2,128)S(1)} %get-tuple-element.137) | copy-start | bytes 18436
  271.3 45.3 %copy-start.36 = (f32[2,768]{1,0:T(2,128)}, f32[2,768]{1,0:T(2,128)S(1)}, u32[]{:S(2)}) copy-start(f32[2,768]{1,0:T(2,128)S(1)} %get-tuple-element.136) | copy-start | bytes 18436
  278.6 9.5 copy-start.19
  278.6 9.5 copy-start.45
  288.1 10.0 copy-start.43
  316.6 9.3 copy-start.40
  325.8 9.2 copy-start.59
  338.8 62.9 %copy-start.34 = (f32[768]{0:T(1024)}, f32[768]{0:T(1024)S(1)}, u32[]{:S(2)}) copy-start(f32[768]{0:T(1024)S(1)} %broadcast_multiply_fusion) | copy-start | bytes 9220
  340.6 61.2 %copy-start.48 = (f32[768]{0:T(1024)}, f32[768]{0:T(1024)S(1)}, u32[]{:S(2)}) copy-start(f32[768]{0:T(1024)S(1)} %fusion.102) | copy-start | bytes 9220
  340.6 34.3 %copy-start.23 = (bf16[1,768,768]{2,1,0:T(8,128)(2,1)S(1)}, bf16[1,768,768]{2,1,0:T(8,128)(2,1)}, u32[]{:S(2)}) copy-start(bf16[1,768,768]{2,1,0:T(8,128)(2,1)} %param.21) | copy-start | bytes 3538948
  374.9 12.5 copy-start.65
  405.2 11.6 slice-start.29
  406.3 10.5 slice-start.30
  440.5 19.3 %slice-start.10 = ((s8[18874368]{0:T(1024)(128)(4,1)}), s8[4194304]{0:T(1024)(128)(4,1)S(1)}, s32[]{:S(2)}) async-start(s8[18874368]{0:T(1024)(128)(4,1)} %bitcast.327), calls=%async_computation.29 | async-start | bytes 8388608
  440.5 19.3 %slice-start.11 = ((s8[18874368]{0:T(1024)(128)(4,1)}), s8[4194304]{0:T(1024)(128)(4,1)S(1)}, s32[]{:S(2)}) async-start(s8[18874368]{0:T(1024)(128)(4,1)} %bitcast.327), calls=%async_computation.30 | async-start | bytes 8388608
  440.5 19.3 %slice-start.12 = ((s8[18874368]{0:T(1024)(128)(4,1)}), s8[4194304]{0:T(1024)(128)(4,1)S(1)}, s32[]{:S(2)}) async-start(s8[18874368]{0:T(1024)(128)(4,1)} %bitcast.327), calls=%async_computation.31 | async-start | bytes 8388608
  450.5 9.3 slice-start.13
  450.5 9.3 slice-start.14
  450.5 9.3 copy-start.46
  466.4 11.3 copy-start.39
  466.4 22.9 %slice-start = ((s8[18874368]{0:T(1024)(128)(4,1)}), s8[4194304]{0:T(1024)(128)(4,1)S(1)}, s32[]{:S(2)}) async-start(s8[18874368]{0:T(1024)(128)(4,1)} %bitcast.323), calls=%async_computation.19 | async-start | bytes 8388608
  466.4 22.9 %slice-start.1 = ((s8[18874368]{0:T(1024)(128)(4,1)}), s8[4194304]{0:T(1024)(128)(4,1)S(1)}, s32[]{:S(2)}) async-start(s8[18874368]{0:T(1024)(128)(4,1)} %bitcast.323), calls=%async_computation.20 | async-start | bytes 8388608
  466.4 22.9 %slice-start.2 = ((s8[18874368]{0:T(1024)(128)(4,1)}), s8[4194304]{0:T(1024)(128)(4,1)S(1)}, s32[]{:S(2)}) async-start(s8[18874368]{0:T(1024)(128)(4,1)} %bitcast.323), calls=%async_computation.21 | async-start | bytes 8388608
  477.8 11.6 slice-start.3
  477.8 11.6 slice-start.4
  477.8 11.6 copy-start.37
  506.4 243.7 %reduce-scatter.8.cloned.1.call-start = ((), (), s32[]{:S(2)}) async-start(), calls=%async_computation.10 | async-start | bytes 5898240 | tf_op jit(solution)/shard_map/reduce_scatter | solution.py:229
  583.0 61.9 %copy-start.13 = (bf16[768,768]{0,1:T(8,128)(2,1)S(1)}, bf16[768,768]{0,1:T(8,128)(2,1)}, u32[]{:S(2)}) copy-start(bf16[768,768]{0,1:T(8,128)(2,1)} %copy-done.12) | copy-start | bytes 3538948
  644.8 11.3 copy-start.1
  650.5 9.9 slice-start.5
  650.5 9.9 slice-start.6
  650.5 9.9 slice-start.7
  689.6 11.0 slice-start.18
  689.6 11.0 slice-start.19
  703.3 192.1 %all-reduce.23.cloned.1.call-start = ((), (), s32[]{:S(2)}) async-start(), calls=%async_computation.18 | async-start | bytes 188416
  703.4 15.8 %slice-start.24 = ((s8[9437184]{0:T(1024)(128)(4,1)}), s8[4194304]{0:T(1024)(128)(4,1)S(1)}, s32[]{:S(2)}) async-start(s8[9437184]{0:T(1024)(128)(4,1)} %bitcast.335), calls=%async_computation.43 | async-start | bytes 8388608
  703.4 15.8 %slice-start.25 = ((s8[9437184]{0:T(1024)(128)(4,1)}), s8[4194304]{0:T(1024)(128)(4,1)S(1)}, s32[]{:S(2)}) async-start(s8[9437184]{0:T(1024)(128)(4,1)} %bitcast.335), calls=%async_computation.44 | async-start | bytes 8388608
  703.4 15.8 %slice-start.27 = ((s8[4718592]{0:T(1024)(128)(4,1)}), s8[4194304]{0:T(1024)(128)(4,1)S(1)}, s32[]{:S(2)}) async-start(s8[4718592]{0:T(1024)(128)(4,1)} %bitcast.345), calls=%async_computation.46 | async-start | bytes 8388608
  710.5 8.7 slice-start.28
  719.2 9.9 slice-start.15
  719.2 9.9 slice-start.16
  722.2 9.9 slice-start.21
  722.2 9.9 slice-start.22
  768.8 233.1 %reduce-scatter.14.cloned.1.call-start = ((), (), s32[]{:S(2)}) async-start(), calls=%async_computation.13 | async-start | bytes 2433024 | tf_op jit(solution)/shard_map/reduce_scatter | solution.py:256
  773.5 369.6 %reduce-scatter.16.cloned.1.call-start = ((), (), s32[]{:S(2)}) async-start(), calls=%async_computation.14 | async-start | bytes 9732096 | tf_op jit(solution)/shard_map/reduce_scatter | solution.py:260
  784.2 500.7 %reduce-scatter.18.cloned.1.call-start = ((), (), s32[]{:S(2)}) async-start(), calls=%async_computation.15 | async-start | bytes 9732096 | tf_op jit(solution)/shard_map/reduce_scatter | solution.py:262
  794.8 614.7 %reduce-scatter.12.cloned.1.call-start = ((), (), s32[]{:S(2)}) async-start(), calls=%async_computation.12 | async-start | bytes 7299072 | tf_op jit(solution)/shard_map/reduce_scatter | solution.py:253
  804.8 9.2 copy-start.50
  (48 other events, 215.6 us)
Sparse Core Ops, SparseCore 0:
  10.9 63.0 all-gather.9
  114.1 33.5 all-gather.19
  149.8 37.4 all-gather.17
  190.1 54.1 all-gather.11
  247.0 62.4 all-gather.13
  312.3 62.5 all-gather.15
  506.6 46.6 reduce-scatter.9
  703.5 46.6 reduce-scatter.7
  769.0 126.4 all-reduce.22
  902.0 99.8 reduce-scatter.13
  1008.4 134.6 reduce-scatter.15
  1150.4 134.4 reduce-scatter.17
  1291.2 118.2 reduce-scatter.11
where the time goes:
time: 1420 us
  waiting for transfers between devices  618 us (44%)
  matrix products  491 us (35%)
  other arithmetic  142 us (10%)
  blocking collectives  83.9 us (6%)
  local copies, waits for them, and re-layouts  64.9 us (5%)
  between operations  15.4 us (1%)
    reduce_scatter x1, waiting for transfers between devices, local(): lax.psum_scatter(grad_down_weight, ('seq', 'freq'), scatter_dimension=0,...  142 us
    reduce_scatter x1, waiting for transfers between devices, local(): lax.psum_scatter(grad_up_weight, ('seq', 'freq'), scatter_dimension=0, ti...  141 us
    reduce_scatter x1, waiting for transfers between devices, local(): lax.psum_scatter(grad_qkv_weight, ('seq', 'freq'), scatter_dimension=0, t...  125 us
    dot_general x6, matrix products, local(): jnp.einsum('sqhe,skhe->shqk', context_piece, all_values[:, :, first_head:...  119 us
    reduce_scatter x1, waiting for transfers between devices, local(): lax.psum_scatter(grad_out_weight, ('seq', 'freq'), scatter_dimension=0, t...  93.8 us
    convert_element_type x2, other arithmetic, local(): (attention_probability_map * (grad_prob - inner_sum)).astype(narrow)  89.6 us
    dot_general x6, matrix products, block_scores(): jnp.einsum('sqhe,skhe->shqk', queries[:, :, first_head:first_head + per_b...  88.6 us
    unnamed x14, waiting for transfers between devices  79.7 us
  transfers between devices with their start and end apart: 13, of which 8 were waited for; matrix products, arithmetic and copies ran while one was open for 37% of the time, Pallas kernels for 0%

commit v1 on v0

v1 whole, which is shorter than its diff:
```python
import functools

import jax
import jax.numpy as jnp
import numpy as np
from jax import lax
from jax.experimental import pallas as pl
from jax.experimental.pallas import tpu as pltpu
from jax.sharding import PartitionSpec as P

HEADS = 12
HEAD_DIM = 64
FREQS = 12
CLIPS = 8
WIN = 128
CHIPS = 16
EPS = 1e-06
MASKED = -1e30
BOTH = ("seq", "freq")
F32 = jnp.float32
BF16 = jnp.bfloat16
VMEM_LIMIT = 60 * 1024 * 1024


def params(**kw):
    return pltpu.CompilerParams(vmem_limit_bytes=VMEM_LIMIT, **kw)


def whole():
    return pl.BlockSpec(memory_space=pltpu.VMEM)


def smem():
    return pl.BlockSpec(memory_space=pltpu.SMEM)


def hbm():
    return pl.BlockSpec(memory_space=pl.ANY)


def once(shape):
    return pl.BlockSpec(shape, lambda *_: (0,) * len(shape), pipeline_mode=pl.Buffered(1))


def mm(a, b):
    return jnp.dot(a, b, preferred_element_type=F32)


def mm_nt(a, b):
    return lax.dot_general(a, b, (((1,), (1,)), ((), ())), preferred_element_type=F32)


def mm_tn(a, b):
    return lax.dot_general(a, b, (((0,), (0,)), ((), ())), preferred_element_type=F32)


def norm_stats(values):
    center = values - jnp.mean(values, axis=-1, keepdims=True)
    spread = jnp.mean(center * center, axis=-1, keepdims=True)
    inv = lax.rsqrt(spread + EPS)
    return center * inv, inv


def norm_back(vhat, inv, dy, gain):
    gd = dy * gain
    return inv * (
        gd
        - jnp.mean(gd, axis=-1, keepdims=True)
        - vhat * jnp.mean(gd * vhat, axis=-1, keepdims=True)
    )


def row_sum(values):
    return jnp.sum(values, axis=0, keepdims=True)


def embed(tokens, ids, ptab):
    hot = (lax.broadcasted_iota(jnp.int32, (16, ids.shape[1]), 0) == ids).astype(BF16)
    return tokens.astype(F32) + mm_tn(hot, ptab[16:32, :].astype(BF16)), hot


def qkv_kernel(
    tab, t0, t1, t2, t3, ids, own, oth, normed, keys, values, queries, hidden, weight, ptab,
    pm, sems, *, rows
):
    step = pl.program_id(0)
    feature = weight.shape[0]
    block = feature // CHIPS
    seg = feature // 2
    core = tab[4, 0]

    def copies(cc):
        made = []
        for r in range(CHIPS):
            for half, ref in ((cc, own), (1 - cc, oth)):
                dst = pl.multiple_of(tab[0 if half == cc else 1, r] * block, 16)
                for n in range(3):
                    made.append(
                        pltpu.make_async_copy(
                            ref.at[pl.ds(r * block, block), pl.ds(n * seg, seg)],
                            weight.at[
                                pl.ds(dst, block), pl.ds(n * feature + half * seg, seg)
                            ],
                            sems.at[len(made)],
                        )
                    )
            made.append(
                pltpu.make_async_copy(
                    own.at[pl.ds(r * block, block), pl.ds(3 * seg, 128)],
                    pm.at[pl.ds(pl.multiple_of(tab[0, r] * block, 16), block), :],
                    sems.at[len(made)],
                )
            )
        return made

    @pl.when(step == 0)
    def _():
        for cc in (0, 1):

            @pl.when(core == cc)
            def _():
                made = copies(cc)
                for one in made:
                    one.start()
                for one in made:
                    one.wait()

        ptab[...] = pm[...].astype(F32).T[:32, :]

    per = keys.shape[0]
    tiles = t0.shape[0]
    steps = 768 // per
    del tiles

    def body(tok, own_rows):
        value, _ = embed(tok[...], ids[0], ptab)
        vhat, _ = norm_stats(value)
        low = (vhat * ptab[0:1, :] + ptab[1:2, :]).astype(BF16)
        normed[...] = low
        if own_rows:
            hidden[...] = value
            q = mm(low, weight[:, 0:feature]) + ptab[2:3, :]
            queries[...] = q.astype(BF16) * jnp.asarray(HEAD_DIM**-0.5, BF16)
        keys[...] = mm(low, weight[:, feature : 2 * feature]).astype(BF16)
        values[...] = (mm(low, weight[:, 2 * feature :]) + ptab[3:4, :]).astype(BF16)

    for piece, tok in enumerate((t0, t1, t2, t3)):

        @pl.when((step >= piece * steps) & (step < (piece + 1) * steps))
        def _():
            body(tok, piece == 0)


def qkv_call(tab, pieces, ids, own, oth):
    group, feature = pieces[0].shape
    per = 256
    steps = group // per
    total = 4 * steps

    def at(piece):
        return pl.BlockSpec(
            (per, feature), lambda i: (jnp.clip(i - piece * steps, 0, steps - 1), 0)
        )

    tile = pl.BlockSpec((per, feature), lambda i: (i, 0))
    first = pl.BlockSpec((per, feature), lambda i: (jnp.minimum(i, steps - 1), 0))
    return pl.pallas_call(
        functools.partial(qkv_kernel, rows=per),
        grid=(total,),
        in_specs=[smem()]
        + [at(p) for p in range(4)]
        + [pl.BlockSpec((1, 1, per), lambda i: (i, 0, 0)), hbm(), hbm()],
        out_specs=[tile, tile, tile, first, first, once((feature, 3 * feature)), once((32, feature))],
        out_shape=[
            jax.ShapeDtypeStruct((4 * group, feature), BF16),
            jax.ShapeDtypeStruct((4 * group, feature), BF16),
            jax.ShapeDtypeStruct((4 * group, feature), BF16),
            jax.ShapeDtypeStruct((group, feature), BF16),
            jax.ShapeDtypeStruct((group, feature), F32),
            jax.ShapeDtypeStruct((feature, 3 * feature), BF16),
            jax.ShapeDtypeStruct((32, feature), F32),
        ],
        scratch_shapes=[
            pltpu.VMEM((feature, 128), BF16),
            pltpu.SemaphoreType.DMA((7 * CHIPS,)),
        ],
        compiler_params=params(),
        cost_estimate=pl.CostEstimate(
            flops=2 * group * feature * feature * 9, bytes_accessed=30_000_000, transcendentals=0
        ),
        name="qkv",
    )(tab, *pieces, ids.reshape(total, 1, per), own, oth)


def window(starts, g, clip, n, group):
    first = starts[g * 16 + clip]
    last = starts[g * 16 + clip + 1]
    lead = (first // 16) * 16 + n * WIN
    base = pl.multiple_of(jnp.minimum(lead, group - WIN), 16)
    return base, jnp.maximum(first, lead) - base, last - base


def counts(starts, clip, groups):
    def need(g):
        first = (starts[g * 16 + clip] // 16) * 16
        return (starts[g * 16 + clip + 1] - first + WIN - 1) // WIN

    spans = [need(g) for g in groups]
    most = spans[0]
    for s in spans[1:]:
        most = jnp.maximum(most, s)
    return most


def lane_halves():
    lane = lax.broadcasted_iota(jnp.int32, (1, 128), 1)
    left = (lane < HEAD_DIM).astype(BF16)
    return left, 1 - left


def stack_heads(rows):
    left, right = lane_halves()
    return jnp.concatenate([rows * left, rows * right], axis=0)


def merge_heads(stacked):
    lane = lax.broadcasted_iota(jnp.int32, (WIN, 128), 1)
    return jnp.where(lane < HEAD_DIM, stacked[:WIN], stacked[WIN:])


def row_valid(lo, hi):
    row = lax.broadcasted_iota(jnp.int32, (WIN, 128), 0)
    return (row >= lo) & (row < hi)


def load_keys(starts, clip, n, group, *refs):
    tiles = [[] for _ in refs]
    spans = []
    for g in range(4):
        base, lo, hi = window(starts, g, clip, n, group)
        for t, ref in zip(tiles, refs):
            t.append(ref[pl.ds(pl.multiple_of(g * group + base, 16), WIN), :])
        spans.append((base, lo, hi))
    return [jnp.concatenate(t, axis=0) for t in tiles], spans


def key_bias_row(spans):
    lane = lax.broadcasted_iota(jnp.int32, (1, WIN), 1)
    return jnp.concatenate(
        [jnp.where((lane >= lo) & (lane < hi), 0.0, MASKED) for _, lo, hi in spans], axis=1
    )


def key_bias_col(spans):
    row = lax.broadcasted_iota(jnp.int32, (WIN, 2 * WIN), 0)
    return jnp.concatenate(
        [jnp.where((row >= lo) & (row < hi), 0.0, MASKED) for _, lo, hi in spans], axis=0
    )


def attn_kernel(starts, q, k, v, out, *, group):
    def one(clip):
        base, lo, hi = window(starts, 0, clip, 0, group)
        stacked = stack_heads(q[pl.ds(base, WIN), :])
        (kt, vt), spans = load_keys(starts, clip, 0, group, k, v)
        scores = mm_nt(stacked, kt) + key_bias_row(spans)
        peak = jnp.max(scores, axis=1, keepdims=True)
        e = jnp.exp(scores - peak)
        total = jnp.sum(e, axis=1, keepdims=True)
        o = mm(e.astype(BF16), vt) * (1.0 / total)
        spot = pl.ds(base, WIN)
        out[spot, :] = jnp.where(row_valid(lo, hi), merge_heads(o).astype(BF16), out[spot, :])

    def many(clip, rows, steps):
        @pl.loop(0, rows)
        def _(i):
            base, lo, hi = window(starts, 0, clip, i, group)
            stacked = stack_heads(q[pl.ds(base, WIN), :])

            def inner(j, carry):
                peak, total, acc = carry
                (kt, vt), spans = load_keys(starts, clip, j, group, k, v)
                scores = mm_nt(stacked, kt) + key_bias_row(spans)
                new = jnp.maximum(peak, jnp.max(scores, axis=1, keepdims=True))
                e = jnp.exp(scores - new)
                shrink = jnp.exp(peak - new)
                return (
                    new,
                    total * shrink + jnp.sum(e, axis=1, keepdims=True),
                    acc * shrink + mm(e.astype(BF16), vt),
                )

            start = (
                jnp.full((2 * WIN, 1), 2 * MASKED, F32),
                jnp.zeros((2 * WIN, 1), F32),
                jnp.zeros((2 * WIN, 128), F32),
            )
            _, total, acc = lax.fori_loop(0, steps, inner, start)
            o = merge_heads(acc * (1.0 / total)).astype(BF16)
            spot = pl.ds(base, WIN)
            out[spot, :] = jnp.where(row_valid(lo, hi), o, out[spot, :])

    most = counts(starts, 0, range(4))
    for clip in range(1, CLIPS):
        most = jnp.maximum(most, counts(starts, clip, range(4)))

    @pl.when(most <= 1)
    def _():
        for clip in range(CLIPS):
            one(clip)

    @pl.when(most > 1)
    def _():
        @pl.loop(0, CLIPS)
        def _(clip):
            many(clip, counts(starts, clip, [0]), counts(starts, clip, range(4)))


def attn_call(starts, queries, keys, values):
    group, feature = queries.shape
    return pl.pallas_call(
        functools.partial(attn_kernel, group=group),
        grid=(feature // 128,),
        in_specs=[
            smem(),
            pl.BlockSpec((group, 128), lambda i: (0, i)),
            pl.BlockSpec((4 * group, 128), lambda i: (0, i)),
            pl.BlockSpec((4 * group, 128), lambda i: (0, i)),
        ],
        out_specs=pl.BlockSpec((group, 128), lambda i: (0, i)),
        out_shape=jax.ShapeDtypeStruct((group, feature), BF16),
        compiler_params=params(),
        cost_estimate=pl.CostEstimate(
            flops=10_000_000_000, bytes_accessed=12_000_000, transcendentals=6_300_000
        ),
        name="attention",
    )(starts, queries, keys, values)


def attn_back_kernel(starts, q, k, v, go, dq, dk, dv, dk_acc, dv_acc, dq_acc, *, group):
    dk_acc[...] = jnp.zeros_like(dk_acc)
    dv_acc[...] = jnp.zeros_like(dv_acc)
    dq_acc[...] = jnp.zeros_like(dq_acc)
    scale = HEAD_DIM**-0.5

    def load_query(clip, i):
        base, lo, hi = window(starts, 0, clip, i, group)
        spot = pl.ds(base, WIN)
        keep = jnp.where(row_valid(lo, hi), go[spot, :], jnp.zeros((), BF16))
        return base, stack_heads(q[spot, :]), stack_heads(keep)

    def finish(spans, base, kt, stacked, back, prob, ds):
        ds = ds.astype(BF16)
        dvt = mm(prob.astype(BF16), back)
        dkt = mm(ds, stacked)
        for g, (kb, _, _) in enumerate(spans):
            spot = pl.ds(pl.multiple_of(g * group + kb, 16), WIN)
            dk_acc[spot, :] += dkt[g * WIN : (g + 1) * WIN]
            dv_acc[spot, :] += dvt[g * WIN : (g + 1) * WIN]
        spot = pl.ds(base, WIN)
        dq_acc[spot, :] += merge_heads(mm_tn(ds, kt))

    def one(clip):
        base, stacked, back = load_query(clip, 0)
        (kt, vt), spans = load_keys(starts, clip, 0, group, k, v)
        scores = mm_nt(kt, stacked) + key_bias_col(spans)
        peak = jnp.max(scores, axis=0, keepdims=True)
        e = jnp.exp(scores - peak)
        prob = e * (1.0 / jnp.sum(e, axis=0, keepdims=True))
        gp = mm_nt(vt, back)
        inner = jnp.sum(prob * gp, axis=0, keepdims=True)
        finish(spans, base, kt, stacked, back, prob, prob * (gp - inner))

    def many(clip, rows, steps):
        @pl.loop(0, rows)
        def _(i):
            base, stacked, back = load_query(clip, i)

            def totals(j, carry):
                peak, total, inner = carry
                (kt, vt), spans = load_keys(starts, clip, j, group, k, v)
                scores = mm_nt(kt, stacked) + key_bias_col(spans)
                new = jnp.maximum(peak, jnp.max(scores, axis=0, keepdims=True))
                e = jnp.exp(scores - new)
                shrink = jnp.exp(peak - new)
                gp = mm_nt(vt, back)
                return (
                    new,
                    total * shrink + jnp.sum(e, axis=0, keepdims=True),
                    inner * shrink + jnp.sum(e * gp, axis=0, keepdims=True),
                )

            zero = jnp.zeros((1, 2 * WIN), F32)
            peak, total, inner = lax.fori_loop(
                0, steps, totals, (jnp.full((1, 2 * WIN), 2 * MASKED, F32), zero, zero)
            )
            part = 1.0 / total
            inner = inner * part

            @pl.loop(0, steps)
            def _(j):
                (kt, vt), spans = load_keys(starts, clip, j, group, k, v)
                scores = mm_nt(kt, stacked) + key_bias_col(spans)
                prob = jnp.exp(scores - peak) * part
                gp = mm_nt(vt, back)
                finish(spans, base, kt, stacked, back, prob, prob * (gp - inner))

    most = counts(starts, 0, range(4))
    for clip in range(1, CLIPS):
        most = jnp.maximum(most, counts(starts, clip, range(4)))

    @pl.when(most <= 1)
    def _():
        for clip in range(CLIPS):
            one(clip)

    @pl.when(most > 1)
    def _():
        @pl.loop(0, CLIPS)
        def _(clip):
            many(clip, counts(starts, clip, [0]), counts(starts, clip, range(4)))

    dq[...] = (dq_acc[...] * scale).astype(BF16)
    dk[...] = dk_acc[...].astype(BF16)
    dv[...] = dv_acc[...].astype(BF16)


def attn_back_call(starts, queries, keys, values, grad_context):
    group, feature = queries.shape
    small = pl.BlockSpec((group, 128), lambda i: (0, i))
    large = pl.BlockSpec((4 * group, 128), lambda i: (0, i))
    return pl.pallas_call(
        functools.partial(attn_back_kernel, group=group),
        grid=(feature // 128,),
        in_specs=[smem(), small, large, large, small],
        out_specs=[small, large, large],
        out_shape=[
            jax.ShapeDtypeStruct((group, feature), BF16),
            jax.ShapeDtypeStruct((4 * group, feature), BF16),
            jax.ShapeDtypeStruct((4 * group, feature), BF16),
        ],
        scratch_shapes=[
            pltpu.VMEM((4 * group, 128), F32),
            pltpu.VMEM((4 * group, 128), F32),
            pltpu.VMEM((group, 128), F32),
        ],
        compiler_params=params(),
        cost_estimate=pl.CostEstimate(
            flops=20_000_000_000, bytes_accessed=24_000_000, transcendentals=6_300_000
        ),
        name="attention_back",
    )(starts, queries, keys, values, grad_context)


def phi_parts(u):
    x = jnp.abs(u) * (0.5**0.5)
    t = 1.0 / (1.0 + 0.3275911 * x)
    e = jnp.exp(-(x * x))
    poly = t * (
        0.254829592
        + t * (-0.284496736 + t * (1.421413741 + t * (-1.453152027 + t * 1.061405429)))
    )
    tail = 0.5 * poly * e
    return jnp.where(u < 0, tail, 1.0 - tail), e * 0.3989422804014327


def middle_kernel(
    tab, ctx, hidden, ups, ptab, up_bias, uo_own, uo_oth, dn_own, dn_oth,
    mixed, grad_mid, grad_ctx, g_uo_own, g_uo_oth, g_dn_own, g_dn_oth, small, g_up_bias,
    w_up, w_dn, w_out, mid, sec, sec_t, acc, gsec, act, gup, t_up, t_dn, in_sems, up_sems, dn_sems,
    *, chunks
):
    j = pl.program_id(0)
    group, feature = ctx.shape
    block = feature // CHIPS
    dblock = w_dn.shape[0] // CHIPS
    seg = feature // 2
    part = w_dn.shape[0] // chunks
    per_half = chunks // 2
    core = tab[4, 0]
    tile = 256
    tiles = group // tile

    def loads(cc):
        made = []

        def add(src, dst):
            made.append(pltpu.make_async_copy(src, dst, in_sems.at[len(made)]))

        for r in range(CHIPS):
            for half, ref, dref, row in ((cc, uo_own, dn_own, 0), (1 - cc, uo_oth, dn_oth, 1)):
                chip = tab[row, r]
                dst = pl.ds(pl.multiple_of(chip * block, 16), block)
                src = pl.ds(r * block, block)
                add(
                    ref.at[src, pl.ds(per_half * part, seg)],
                    w_out.at[dst, pl.ds(half * seg, seg)],
                )
                for n in range(per_half):
                    add(
                        ref.at[src, pl.ds(n * part, part)],
                        w_up.at[half * per_half + n, dst, :],
                    )
                add(
                    dref.at[pl.ds(r * dblock, dblock), :],
                    w_dn.at[
                        pl.ds(pl.multiple_of(chip * dblock, 16), dblock), pl.ds(half * seg, seg)
                    ],
                )
        return made

    def for_core(run):
        for cc in (0, 1):

            @pl.when(core == cc)
            def _():
                run(cc)

    @pl.when(j == 0)
    def _():
        def run(cc):
            made = loads(cc)
            for one in made:
                one.start()
            for one in made:
                one.wait()

        for_core(run)
        for t in range(tiles):
            rows = slice(t * tile, (t + 1) * tile)
            value = hidden[rows, :] + mm(ctx[rows, :], w_out[...]) + ptab[4:5, :]
            mid[rows, :] = value
            vhat, _ = norm_stats(value)
            low = (vhat * ptab[5:6, :] + ptab[6:7, :]).astype(BF16)
            sec[rows, :] = low
            sec_t[:, rows] = low.T
            acc[rows, :] = value + ptab[7:8, :]
            gsec[rows, :] = jnp.zeros((tile, feature), F32)

    slot = lax.rem(j, 2)

    def up_stores(jj, sl, cc):
        own = (jj // per_half) == cc
        made = []
        for r in range(CHIPS):
            made.append((r, own))
        return made

    def drain(sl):
        for r in range(CHIPS):
            pltpu.make_async_copy(
                t_up.at[sl, pl.ds(0, block), :],
                g_uo_own.at[pl.ds(0, block), pl.ds(0, part)],
                up_sems.at[sl, r],
            ).wait()
        for n in range(2 * (part // dblock)):
            pltpu.make_async_copy(
                t_dn.at[sl, pl.ds(0, dblock), pl.ds(0, seg)],
                g_dn_own.at[pl.ds(0, dblock), :],
                dn_sems.at[sl, n],
            ).wait()

    del up_stores

    upj = w_up[j]
    dnj = w_dn[pl.ds(pl.multiple_of(j * part, 128), part), :]
    bias = up_bias[pl.ds(j, 1), :]
    gub = jnp.zeros((1, part), F32)
    for t in range(tiles):
        rows = slice(t * tile, (t + 1) * tile)
        u = mm(sec[rows, :], upj) + bias
        dist, dens = phi_parts(u)
        a = (u * dist).astype(BF16)
        g = (mm_nt(ups[rows, :], dnj) * (dist + u * dens)).astype(BF16)
        act[rows, :] = a
        gup[rows, :] = g
        gub = gub + row_sum(g.astype(F32))
        acc[rows, :] += mm(a, dnj)
        gsec[rows, :] += mm_nt(g, upj)
    g_up_bias[pl.ds(j, 1), :] = gub

    @pl.when(j >= 2)
    def _():
        drain(slot)

    t_up[slot] = mm(sec_t[...], gup[...]).astype(BF16)
    t_dn[slot] = mm_tn(act[...], ups[...]).astype(BF16)

    def send(cc):
        col = pl.ds(pl.multiple_of(lax.rem(j, per_half) * part, 128), part)
        for is_own in (True, False):
            ref = g_uo_own if is_own else g_uo_oth

            @pl.when((j // per_half == cc) == is_own)
            def _():
                for r in range(CHIPS):
                    src = pl.ds(pl.multiple_of(tab[0 if is_own else 1, r] * block, 16), block)
                    pltpu.make_async_copy(
                        t_up.at[slot, src, :],
                        ref.at[pl.ds(r * block, block), col],
                        up_sems.at[slot, r],
                    ).start()

        n = 0
        count = part // dblock
        for half, ref, row in ((cc, g_dn_own, 2), (1 - cc, g_dn_oth, 3)):
            for i in range(count):
                place = tab[row, j * count + i]
                pltpu.make_async_copy(
                    t_dn.at[slot, pl.ds(i * dblock, dblock), pl.ds(half * seg, seg)],
                    ref.at[pl.ds(pl.multiple_of(place * dblock, 16), dblock), :],
                    dn_sems.at[slot, n],
                ).start()
                n += 1

    for_core(send)

    @pl.when(j == chunks - 1)
    def _():
        s_gain = jnp.zeros((1, feature), F32)
        s_shift = jnp.zeros((1, feature), F32)
        s_out = jnp.zeros((1, feature), F32)
        s_down = jnp.zeros((1, feature), F32)
        for t in range(tiles):
            rows = slice(t * tile, (t + 1) * tile)
            mixed[rows, :] = acc[rows, :].astype(BF16)
            vhat, inv = norm_stats(mid[rows, :])
            dy = gsec[rows, :]
            wide = ups[rows, :].astype(F32)
            gm = wide + norm_back(vhat, inv, dy, ptab[5:6, :])
            grad_mid[rows, :] = gm
            low = gm.astype(BF16)
            gup[rows, :] = low
            grad_ctx[rows, :] = mm_nt(low, w_out[...]).astype(BF16)
            s_gain = s_gain + row_sum(dy * vhat)
            s_shift = s_shift + row_sum(dy)
            s_out = s_out + row_sum(gm)
            s_down = s_down + row_sum(wide)
        zero = jnp.zeros((1, feature), F32)
        small[...] = jnp.concatenate(
            [zero, zero, zero, zero, s_out, s_gain, s_shift, s_down], axis=0
        )
        drain(1 - slot)
        act[...] = mm_tn(ctx[...], gup[...]).astype(BF16)

        def run(cc):
            made = []
            for half, ref, row in ((cc, g_uo_own, 0), (1 - cc, g_uo_oth, 1)):
                for r in range(CHIPS):
                    src = pl.ds(pl.multiple_of(tab[row, r] * block, 16), block)
                    made.append(
                        pltpu.make_async_copy(
                            act.at[src, pl.ds(half * seg, seg)],
                            ref.at[pl.ds(r * block, block), pl.ds(per_half * part, seg)],
                            in_sems.at[len(made)],
                        )
                    )
            for one in made:
                one.start()
            for one in made:
                one.wait()

        for_core(run)
        drain(slot)


def middle_call(tab, ctx, hidden, ups, ptab, up_bias, uo, dn):
    group, feature = ctx.shape
    ff = dn[0].shape[0]
    chunks = ff // feature
    part = ff // chunks
    half_uo = uo[0].shape[1]
    return pl.pallas_call(
        functools.partial(middle_kernel, chunks=chunks),
        grid=(chunks,),
        in_specs=[
            smem(),
            once((group, feature)),
            once((group, feature)),
            once((group, feature)),
            once((32, feature)),
            once((chunks, part)),
            hbm(), hbm(), hbm(), hbm(),
        ],
        out_specs=[
            once((group, feature)),
            once((group, feature)),
            once((group, feature)),
            hbm(), hbm(), hbm(), hbm(),
            once((8, feature)),
            once((chunks, part)),
        ],
        out_shape=[
            jax.ShapeDtypeStruct((group, feature), BF16),
            jax.ShapeDtypeStruct((group, feature), F32),
            jax.ShapeDtypeStruct((group, feature), BF16),
            jax.ShapeDtypeStruct((feature, half_uo), BF16),
            jax.ShapeDtypeStruct((feature, half_uo), BF16),
            jax.ShapeDtypeStruct((ff, feature // 2), BF16),
            jax.ShapeDtypeStruct((ff, feature // 2), BF16),
            jax.ShapeDtypeStruct((8, feature), F32),
            jax.ShapeDtypeStruct((chunks, part), F32),
        ],
        scratch_shapes=[
            pltpu.VMEM((chunks, feature, part), BF16),
            pltpu.VMEM((ff, feature), BF16),
            pltpu.VMEM((feature, feature), BF16),
            pltpu.VMEM((group, feature), F32),
            pltpu.VMEM((group, feature), BF16),
            pltpu.VMEM((feature, group), BF16),
            pltpu.VMEM((group, feature), F32),
            pltpu.VMEM((group, feature), F32),
            pltpu.VMEM((group, part), BF16),
            pltpu.VMEM((group, part), BF16),
            pltpu.VMEM((2, feature, part), BF16),
            pltpu.VMEM((2, part, feature), BF16),
            pltpu.SemaphoreType.DMA((2 * CHIPS * (2 + chunks // 2),)),
            pltpu.SemaphoreType.DMA((2, CHIPS)),
            pltpu.SemaphoreType.DMA((2, 2 * (part * CHIPS // ff))),
        ],
        compiler_params=params(),
        cost_estimate=pl.CostEstimate(
            flops=2 * group * feature * (3 * feature + 6 * ff),
            bytes_accessed=34_000_000,
            transcendentals=2 * group * ff,
        ),
        name="middle",
    )(tab, ctx, hidden, ups, ptab, up_bias, *uo, *dn)


def qkv_weight_kernel(tab, normed, dq, dk, dv, own, oth, norm_t, tmp, sems):
    total, feature = normed.shape
    group = dq.shape[0]
    block = feature // CHIPS
    seg = feature // 2
    core = tab[4, 0]
    tile = 256
    for t in range(total // tile):
        rows = slice(t * tile, (t + 1) * tile)
        norm_t[:, rows] = normed[rows, :].T

    def stores(cc, n):
        made = []
        for half, ref, row in ((cc, own, 0), (1 - cc, oth, 1)):
            for r in range(CHIPS):
                src = pl.ds(pl.multiple_of(tab[row, r] * block, 16), block)
                made.append(
                    pltpu.make_async_copy(
                        tmp.at[n, src, pl.ds(half * seg, seg)],
                        ref.at[pl.ds(r * block, block), pl.ds(n * seg, seg)],
                        sems.at[n, len(made)],
                    )
                )
        return made

    def on_core(run):
        for cc in (0, 1):

            @pl.when(core == cc)
            def _():
                run(cc)

    def start(n):
        def run(cc):
            for one in stores(cc, n):
                one.start()

        on_core(run)

    cut = 256
    for c0 in range(0, feature, cut):
        cols = slice(c0, c0 + cut)
        tmp[1, :, cols] = mm(norm_t[...], dk[:, cols]).astype(BF16)
    start(1)
    for c0 in range(0, feature, cut):
        cols = slice(c0, c0 + cut)
        tmp[2, :, cols] = mm(norm_t[...], dv[:, cols]).astype(BF16)
    start(2)
    tmp[0] = mm(norm_t[:, :group], dq[...]).astype(BF16)
    start(0)

    def finish(cc):
        for n in range(3):
            for one in stores(cc, n):
                one.wait()

    on_core(finish)


def qkv_weight_call(tab, normed, dq, dk, dv):
    total, feature = normed.shape
    half = 3 * feature // 2
    return pl.pallas_call(
        qkv_weight_kernel,
        in_specs=[smem()] + [whole()] * 4,
        out_specs=[hbm(), hbm()],
        out_shape=[jax.ShapeDtypeStruct((feature, half), BF16)] * 2,
        scratch_shapes=[
            pltpu.VMEM((feature, total), BF16),
            pltpu.VMEM((3, feature, feature), BF16),
            pltpu.SemaphoreType.DMA((3, 2 * CHIPS)),
        ],
        compiler_params=params(),
        cost_estimate=pl.CostEstimate(
            flops=2 * dq.shape[0] * feature * feature * 9,
            bytes_accessed=20_000_000,
            transcendentals=0,
        ),
        name="qkv_weight",
    )(tab, normed, dq, dk, dv)


def qkv_back_kernel(
    tab, t0, t1, t2, t3, ids, dq, dk, dv, gm, weight, ptab, given, out, own, sums, rel, sem
):
    step = pl.program_id(0)
    feature = weight.shape[0]
    steps = 768 // out.shape[0]
    block = feature // CHIPS
    core = tab[4, 0]

    @pl.when(step == 0)
    def _():
        sums[...] = jnp.zeros_like(sums)
        sums[4:12, :] = given[4:12, :]

    def body(tok, own_rows):
        value, hot = embed(tok[...], ids[0], ptab)
        vhat, inv = norm_stats(value)
        dy = mm_nt(dk[...], weight[:, feature : 2 * feature]) + mm_nt(
            dv[...], weight[:, 2 * feature :]
        )
        if own_rows:
            dy = dy + mm_nt(dq[...], weight[:, 0:feature])
            sums[2:3, :] += row_sum(dq[...].astype(F32))
        grad = norm_back(vhat, inv, dy, ptab[0:1, :])
        out[...] = grad.astype(BF16)
        sums[0:1, :] += row_sum(dy * vhat)
        sums[1:2, :] += row_sum(dy)
        sums[3:4, :] += row_sum(dv[...].astype(F32))
        if own_rows:
            grad = grad + gm[...]
        high = grad.astype(BF16)
        rest = (grad - high.astype(F32)).astype(BF16)
        sums[16:32, :] += mm(hot, high) + mm(hot, rest)

    for piece, tok in enumerate((t0, t1, t2, t3)):

        @pl.when((step >= piece * steps) & (step < (piece + 1) * steps))
        def _():
            body(tok, piece == 0)

    @pl.when(step == 4 * steps - 1)
    def _():
        turned = jnp.concatenate([sums[...], jnp.zeros((96, feature), F32)], axis=0).T
        rel[...] = turned.astype(BF16)
        made = []
        for side in range(2):
            for r in range(CHIPS):
                src = pl.ds(pl.multiple_of(tab[side, r] * block, 16), block)
                made.append(
                    pltpu.make_async_copy(
                        rel.at[src, :], own.at[side, pl.ds(r * block, block), :], sem.at[side, r]
                    )
                )
        for one in made:
            one.start()
        for one in made:
            one.wait()

    del core


def qkv_back_call(tab, pieces, ids, dq, dk, dv, gm, weight, ptab, given):
    group, feature = dq.shape
    per = 256
    steps = group // per
    total = 4 * steps

    def at(piece):
        return pl.BlockSpec(
            (per, feature), lambda i: (jnp.clip(i - piece * steps, 0, steps - 1), 0)
        )

    tile = pl.BlockSpec((per, feature), lambda i: (i, 0))
    first = pl.BlockSpec((per, feature), lambda i: (jnp.minimum(i, steps - 1), 0))
    return pl.pallas_call(
        qkv_back_kernel,
        grid=(total,),
        in_specs=[smem()]
        + [at(p) for p in range(4)]
        + [
            pl.BlockSpec((1, 1, per), lambda i: (i, 0, 0)),
            first,
            tile,
            tile,
            first,
            once((feature, 3 * feature)),
            once((32, feature)),
            once((16, feature)),
        ],
        out_specs=[tile, hbm()],
        out_shape=[
            jax.ShapeDtypeStruct((4 * group, feature), BF16),
            jax.ShapeDtypeStruct((2, feature, 128), BF16),
        ],
        scratch_shapes=[
            pltpu.VMEM((32, feature), F32),
            pltpu.VMEM((feature, 128), BF16),
            pltpu.SemaphoreType.DMA((2, CHIPS)),
        ],
        compiler_params=params(),
        cost_estimate=pl.CostEstimate(
            flops=2 * group * feature * feature * 9, bytes_accessed=30_000_000, transcendentals=0
        ),
        name="qkv_back",
    )(tab, *pieces, ids.reshape(total, 1, per), dq, dk, dv, gm, weight, ptab, given)


class Hops:
    def __init__(self, n_seq, n_freq):
        self.n_seq, self.n_freq = n_seq, n_freq
        self.swaps = n_seq == 8 and n_freq == 4
        self.core = lax.axis_index("freq") % 2
        chip = lax.axis_index("seq") * 2 + lax.axis_index("freq") // 2
        ident = np.arange(CHIPS)
        if self.swaps:
            bits = ((4, 8, 2, 1), (4, 8, 1, 2))
            masks = np.zeros((2, CHIPS), np.int32)
            for c in (0, 1):
                for r in range(CHIPS):
                    for b in range(4):
                        if r >> b & 1:
                            masks[c, r] ^= bits[c][b]
            inverse = np.argsort(masks, axis=1).astype(np.int32)
            one, two = jnp.asarray(masks[0]), jnp.asarray(masks[1])
            mine = jnp.where(self.core == 0, one, two) ^ chip
            theirs = jnp.where(self.core == 0, two, one) ^ chip

            def places(order):
                rows = (order[:, None] == jnp.arange(CHIPS)[None, :]).astype(jnp.int32)
                return jnp.sum(rows * jnp.arange(CHIPS, dtype=jnp.int32)[:, None], axis=0)

            del inverse
            rows = [mine, theirs, places(mine), places(theirs)]
        else:
            rows = [jnp.asarray(ident, jnp.int32)] * 4
        rows = [r.astype(jnp.int32) for r in rows]
        rows += [jnp.full((CHIPS,), self.core, jnp.int32)] + [rows[0]] * 3
        self.table = jnp.stack(rows)

    def swap(self, values, move):
        pairs = []
        for s in range(self.n_seq):
            for f in range(self.n_freq):
                ds, df = move(f % 2)
                pairs.append((s * self.n_freq + f, (s ^ ds) * self.n_freq + (f ^ df)))
        return lax.ppermute(values, BOTH, pairs)

    def swap_core(self, values):
        return self.swap(values, lambda c: (0, 1))

    def swap_y(self, values):
        return self.swap(values, lambda c: (0, 2))

    STEPS = (
        lambda c: (2, 0),
        lambda c: (4, 0),
        lambda c: (1, 0) if c == 0 else (0, 2),
        lambda c: (0, 2) if c == 0 else (1, 0),
    )

    def gather(self, shard):
        rows, cols = shard.shape
        half = cols // 2
        if not self.swaps:
            full = lax.all_gather(shard, BOTH, axis=0, tiled=True)
            return (
                lax.dynamic_slice_in_dim(full, self.core * half, half, 1),
                lax.dynamic_slice_in_dim(full, (1 - self.core) * half, half, 1),
            )
        left, right = shard[:, :half], shard[:, half:]
        first = self.core == 0
        mine = jnp.where(first, left, right)
        got = self.swap_core(jnp.where(first, right, left))
        held = jnp.concatenate(
            [jnp.where(first, mine, got), jnp.where(first, got, mine)], axis=0
        )
        for move in self.STEPS:
            held = jnp.concatenate([held, self.swap(held, move)], axis=0)
        return held, self.swap_core(held)

    def scatter(self, own, other):
        rows, half = own.shape
        shard = rows // (self.n_seq * self.n_freq)
        first = self.core == 0
        if not self.swaps:
            left = jnp.where(first, own, other)
            right = jnp.where(first, other, own)
            full = jnp.concatenate([left, right], axis=1).astype(F32)
            return lax.psum_scatter(full, BOTH, scatter_dimension=0, tiled=True)

        def add(a, b):
            return (a.astype(F32) + b.astype(F32)).astype(BF16)

        got = self.swap_core(other)
        for n, move in enumerate(self.STEPS[::-1]):
            cut = own.shape[0] // 2
            send = add(own[cut:], got[cut:])
            own = add(own[:cut], got[:cut])
            got = self.swap(send, move)
        whole_rows = own.astype(F32) + got.astype(F32)
        upper, lower = whole_rows[:shard], whole_rows[shard:]
        mine = jnp.where(first, upper, lower)
        got = self.swap_core(jnp.where(first, lower, upper).astype(BF16)).astype(F32)
        return jnp.concatenate(
            [jnp.where(first, mine, got), jnp.where(first, got, mine)], axis=1
        )


def local(
    tokens,
    freq_ids,
    clip_ids,
    cotangent,
    ln1_gain,
    first_norm_bias,
    qkv_weight,
    q_bias,
    v_bias,
    out_weight,
    out_bias,
    ln2_gain,
    ln2_bias,
    up_weight,
    up_bias,
    down_weight,
    down_bias,
    freq_table,
    *,
    n_seq,
    n_freq,
):
    _, group, feature = tokens.shape
    rd = qkv_weight.shape[0]
    n_dev = n_seq * n_freq
    seg = feature // 2
    ff = up_weight.shape[1]
    hops = Hops(n_seq, n_freq)
    tab = hops.table

    tok = tokens.reshape(group, feature)
    ids = freq_ids.reshape(1, group)
    tok_y, ids_y = hops.swap_y(tok), hops.swap_y(ids)
    tok_c, ids_c = hops.swap_core(tok), hops.swap_core(ids)
    tok_yc, ids_yc = hops.swap_core(tok_y), hops.swap_core(ids_y)
    pieces = (tok, tok_y, tok_c, tok_yc)
    all_ids = jnp.concatenate([ids, ids_y, ids_c, ids_yc], axis=0)

    vectors = [ln1_gain, first_norm_bias, q_bias, v_bias, out_bias, ln2_gain, ln2_bias, down_bias]
    small = jnp.concatenate(
        [vec[:, None] for vec in vectors]
        + [up_bias.reshape(4, rd).T, jnp.zeros((rd, 4), BF16), freq_table]
        + [jnp.zeros((rd, 100), BF16)],
        axis=1,
    )

    def halves(*arrays):
        left = [a[:, : a.shape[1] // 2] for a in arrays]
        right = [a[:, a.shape[1] // 2 :] for a in arrays]
        return left, right

    left, right = halves(
        qkv_weight[:, :feature], qkv_weight[:, feature : 2 * feature], qkv_weight[:, 2 * feature :]
    )
    qkv_pair = hops.gather(jnp.concatenate(left + [small] + right + [small], axis=1))
    left, right = halves(up_weight, out_weight)
    uo_pair = hops.gather(jnp.concatenate(left + right, axis=1))
    dn_pair = hops.gather(down_weight)

    place = lax.axis_index("freq")
    order = jnp.stack([place, place ^ 2, place ^ 1, place ^ 3])
    below = clip_ids.reshape(n_freq, group)[:, None, :] < jnp.arange(16, dtype=jnp.int32)[None, :, None]
    first_rows = jnp.sum(below.astype(jnp.int32), axis=2)
    pick = (order[:, None] == jnp.arange(n_freq)[None, :]).astype(jnp.int32)
    starts = jnp.sum(pick[:, :, None] * first_rows[None, :, :], axis=1).reshape(4 * 16)

    normed, keys, values, queries, hidden, w_qkv, ptab = qkv_call(tab, pieces, all_ids, *qkv_pair)
    context = attn_call(starts, queries, keys, values)
    up_rows = ptab[8:12].reshape(4, n_dev, rd).transpose(1, 0, 2).reshape(ff // feature, feature)
    upstream = cotangent.reshape(group, feature)
    mixed, grad_mid, grad_ctx, g_uo_own, g_uo_oth, g_dn_own, g_dn_oth, sums, g_up_bias = middle_call(
        tab, context, hidden, upstream, ptab, up_rows, uo_pair, dn_pair
    )
    g_dn = hops.scatter(g_dn_own, g_dn_oth)
    g_uo = hops.scatter(g_uo_own, g_uo_oth)
    dq, dk, dv = attn_back_call(starts, queries, keys, values, grad_ctx)
    g_qkv = hops.scatter(*qkv_weight_call(tab, normed, dq, dk, dv))
    given = jnp.concatenate(
        [
            sums,
            g_up_bias.reshape(n_dev, 4, rd).transpose(1, 0, 2).reshape(4, feature),
            jnp.zeros((4, feature), F32),
        ],
        axis=0,
    )
    back, g_small = qkv_back_call(
        tab, pieces, all_ids, dq, dk, dv, grad_mid, w_qkv, ptab, given
    )
    vecs = hops.scatter(g_small[0], g_small[1])

    near = hops.swap_core(back[2 * group :])
    far = (back[group : 2 * group].astype(F32) + near[group:].astype(F32)).astype(BF16)
    far = hops.swap_y(far)
    input_grad = grad_mid + back[:group].astype(F32) + near[:group].astype(F32) + far.astype(F32)

    vecs = vecs[:, :128]
    n_up = ff // 2
    grad_qkv = jnp.concatenate(
        [g_qkv[:, n * seg + h * 3 * seg : (n + 1) * seg + h * 3 * seg] for n in range(3) for h in (0, 1)],
        axis=1,
    )
    grad_up = jnp.concatenate([g_uo[:, :n_up], g_uo[:, n_up + seg : 2 * n_up + seg]], axis=1)
    grad_out = jnp.concatenate([g_uo[:, n_up : n_up + seg], g_uo[:, 2 * n_up + seg :]], axis=1)
    return (
        mixed.reshape(tokens.shape),
        input_grad.astype(BF16).reshape(tokens.shape),
        vecs[:, 0],
        vecs[:, 1],
        grad_qkv,
        vecs[:, 2],
        vecs[:, 3],
        grad_out,
        vecs[:, 4],
        vecs[:, 5],
        vecs[:, 6],
        grad_up,
        vecs[:, 8:12].T.reshape(4 * rd),
        g_dn,
        vecs[:, 7],
        vecs[:, 16 : 16 + FREQS],
    )


def solution(mesh):
    rows = P(BOTH)
    mat = P(BOTH, None)
    act = P("seq", "freq", None)
    in_specs = (
        act, P("seq", "freq"), P("seq", None), act,
        rows, rows, mat, rows, rows, mat, rows, rows, rows, mat, rows, mat, rows, mat,
    )
    out_specs = (
        act, act, rows, rows, mat, rows, rows, mat, rows, rows, rows, mat, rows, mat, rows, mat,
    )
    body = functools.partial(local, n_seq=mesh.shape["seq"], n_freq=mesh.shape["freq"])
    return jax.shard_map(body, mesh=mesh, in_specs=in_specs, out_specs=out_specs, check_vma=False)
```

time: 1420 us -> 546 us (0.38)
  matrix products: 491 us -> 0 us
  waiting for transfers between devices: 618 us -> 195 us
  Pallas kernels: 0 us -> 176 us
  other arithmetic: 142 us -> 21.9 us
  starting transfers between devices: 1.2 us -> 114 us
  blocking collectives: 83.9 us -> 0 us
  local copies, waits for them, and re-layouts: 64.9 us -> 33.1 us
    reduce_scatter x6 -> x0, waiting for transfers between devices: 515 us -> none  [the longest x1 142 us: local(): lax.psum_scatter(grad_down_weight, ('seq', 'freq'), scatter_dimension=0,...]
    dot_general x50 -> x0, matrix products: 491 us -> none  [the longest x6 119 us: local(): jnp.einsum('sqhe,skhe->shqk', context_piece, all_values[:, :, first_head:...]
    ppermute x0 -> x50, waiting for transfers between devices: none -> 195 us  [swap(): return lax.ppermute(values, BOTH, pairs)]
    pallas_call x0 -> x6, Pallas kernels: none -> 176 us  [the longest x1 46.5 us: middle_call(): pl.pallas_call(functools.partial(middle_kernel, chunks=chunks), grid=(chu...]
    ppermute x0 -> x50, starting transfers between devices: none -> 114 us  [swap(): return lax.ppermute(values, BOTH, pairs)]
    convert_element_type x12 -> x22, other arithmetic: 96.5 us -> 10.7 us  [the longest x16 8.95 us: add(): return (a.astype(F32) + b.astype(F32)).astype(BF16)]
    unnamed x14 -> x0, waiting for transfers between devices: 79.7 us -> none
    unnamed x1 -> x0, blocking collectives: 42.7 us -> none
  transfers between devices with their start and end apart: 13 -> 50, of which waited for: 8 -> 22; matrix products, arithmetic and copies ran while one was open for 37% -> 9% of each run, Pallas kernels for 0% -> 13%
where the time goes in v1:
time: 546 us; the launch traced here: 541 us
  waiting for transfers between devices  195 us (36%)
  Pallas kernels  176 us (32%)
  starting transfers between devices  114 us (21%)
  local copies, waits for them, and re-layouts  33.1 us (6%)
  other arithmetic  21.9 us (4%)
    ppermute x50, waiting for transfers between devices, swap(): return lax.ppermute(values, BOTH, pairs)  195 us
    ppermute x50, starting transfers between devices, swap(): return lax.ppermute(values, BOTH, pairs)  114 us
    pallas_call x1, Pallas kernels, middle_call(): pl.pallas_call(functools.partial(middle_kernel, chunks=chunks), grid=(chu...  46.5 us
    pallas_call x1, Pallas kernels, attn_back_call(): pl.pallas_call(functools.partial(attn_back_kernel, group=group), grid=(fe...  37.6 us
    pallas_call x1, Pallas kernels, qkv_back_call(): pl.pallas_call(qkv_back_kernel, grid=(total,), in_specs=[smem()] + [at(p)...  26.6 us
    pallas_call x1, Pallas kernels, qkv_call(): pl.pallas_call(functools.partial(qkv_kernel, rows=per), grid=(total,), in...  25.3 us
    pallas_call x1, Pallas kernels, attn_call(): pl.pallas_call(functools.partial(attn_kernel, group=group), grid=(feature...  20.3 us
    pallas_call x1, Pallas kernels, qkv_weight_call(): pl.pallas_call(qkv_weight_kernel, in_specs=[smem()] + [whole()] * 4, out_...  19.3 us
  transfers between devices with their start and end apart: 50, of which 22 were waited for; matrix products, arithmetic and copies ran while one was open for 9% of the time, Pallas kernels for 13%

profile of v1, /device:TPU:0, one launch (start us, length us, event | category | flops | bytes accessed | tf_op | source)
XLA Modules:
  0.0 541.4 jit_solution(8750730007127262872)
XLA Ops:
  0.7 1.0 broadcast_select_fusion.6
  11.0 0.9 fusion.6
  13.9 2.7 collective-permute-start.7
  20.0 2.1 collective-permute-start.13
  22.1 2.7 collective-permute-start.8
  25.5 2.5 collective-permute-start.20
  28.0 5.8 %collective-permute-done.13 = bf16[48,1920]{1,0:T(8,128)(2,1)S(1)} collective-permute-done((bf16[48,1920]{1,0:T(8,128)(2,1)S(1)}, bf16[48,1920]{1,0:T(8,128)(2,1)S(1)}, u32[]{:S(2)}, u32[]{:S(2)}) %collective-permute-start.13) | collective-permute-done | bytes 184352 | tf_op jit(solution)/shard_map/ppermute | solution.py:958
  34.6 16.8 %collective-permute-done.8 = bf16[96,1280]{1,0:T(8,128)(2,1)S(1)} collective-permute-done((bf16[96,1280]{1,0:T(8,128)(2,1)S(1)}, bf16[96,1280]{1,0:T(8,128)(2,1)S(1)}, u32[]{:S(2)}, u32[]{:S(2)}) %collective-permute-start.8) | collective-permute-done | bytes 245792 | tf_op jit(solution)/shard_map/ppermute | solution.py:958
  51.5 1.6 collective-permute-start.9
  53.1 11.3 %collective-permute-done.14 = bf16[96,1920]{1,0:T(8,128)(2,1)S(1)} collective-permute-done((bf16[96,1920]{1,0:T(8,128)(2,1)S(1)}, bf16[96,1920]{1,0:T(8,128)(2,1)S(1)}, u32[]{:S(2)}, u32[]{:S(2)}) %collective-permute-start.14) | collective-permute-done | bytes 368672 | tf_op jit(solution)/shard_map/ppermute | solution.py:958
  64.4 1.6 collective-permute-start.15
  68.4 1.5 collective-permute-start.10
  69.9 12.4 %collective-permute-done.15 = bf16[192,1920]{1,0:T(8,128)(2,1)S(1)} collective-permute-done((bf16[192,1920]{1,0:T(8,128)(2,1)S(1)}, bf16[192,1920]{1,0:T(8,128)(2,1)S(1)}, u32[]{:S(2)}, u32[]{:S(2)}) %collective-permute-start.15) | collective-permute-done | bytes 737312 | tf_op jit(solution)/shard_map/ppermute | solution.py:958
  82.3 1.0 constant_dynamic-update-slice_fusion.11
  83.3 2.7 collective-permute-start.16
  86.0 1.6 collective-permute-start.21
  89.1 13.2 %collective-permute-done.21 = bf16[768,384]{1,0:T(8,128)(2,1)S(1)} collective-permute-done((bf16[768,384]{1,0:T(8,128)(2,1)S(1)}, bf16[768,384]{1,0:T(8,128)(2,1)S(1)}, u32[]{:S(2)}, u32[]{:S(2)}) %collective-permute-start.21) | collective-permute-done | bytes 589856 | tf_op jit(solution)/shard_map/ppermute | solution.py:958
  102.4 0.9 constant_dynamic-update-slice_fusion.22
  103.3 1.1 constant_dynamic-update-slice_fusion.5.own
  105.0 1.4 collective-permute-start.3
  106.4 12.7 %collective-permute-done.16 = bf16[384,1920]{1,0:T(8,128)(2,1)S(1)} collective-permute-done((bf16[384,1920]{1,0:T(8,128)(2,1)}, bf16[384,1920]{1,0:T(8,128)(2,1)S(1)}, u32[]{:S(2)}, u32[]{:S(2)}) %collective-permute-start.16) | collective-permute-done | bytes 1474592 | tf_op jit(solution)/shard_map/ppermute | solution.py:958
  119.1 1.2 constant_dynamic-update-slice_fusion.16.uo_own
  120.4 24.1 %collective-permute-done.3 = s32[1,768]{1,0:T(1,128)S(1)} collective-permute-done((s32[1,768]{1,0:T(1,128)S(1)}, s32[1,768]{1,0:T(1,128)S(1)}, u32[]{:S(2)}, u32[]{:S(2)}) %collective-permute-start.3) | collective-permute-done | bytes 3104 | tf_op jit(solution)/shard_map/ppermute | solution.py:958
  146.8 1.1 constant_dynamic-update-slice_fusion.27.dn_own
  148.0 0.9 collective-permute-done.5
  151.3 1.0 copy-done.14
  152.3 25.3 %qkv.1 = (bf16[3072,768]{1,0:T(8,128)(2,1)}, bf16[3072,768]{1,0:T(8,128)(2,1)}, bf16[3072,768]{1,0:T(8,128)(2,1)}, bf16[768,768]{1,0:T(8,128)(2,1)}, f32[768,768...) custom-call(s32[8,16]{1,0:T(8,128)} %stack.37.tab, bf16[768,768]{1,0:T(8,128)(2,1)} %bitcast.8.t0, ...), custom_call_target="tpu_custom_call" | custom-call | flops 8153726976 | bytes 30000000 | tf_op jit(solution)/shard_map/qkv/pallas_call | solution.py:167
  179.3 20.3 %attention.1.ctx = bf16[768,768]{1,0:T(8,128)(2,1)} custom-call(s32[64]{0:T(128)} %reshape.101.starts, bf16[768,768]{1,0:T(8,128)(2,1)} %get-tuple-element.39.q, bf16[3072,768]{1,0:T(8,128)(2,1)} %get-tuple-element.40.k, bf16[3072,768]{1,0:T(8,128)(2,1)} %get-tuple-element.41.v), custom_call_target="tpu_custom_call" | custom-call | flops 10000000000 | bytes 12000000 | tf_op jit(solution)/shard_map/attention/pallas_call | solution.py:321
  199.6 46.5 %middle.1 = (bf16[768,768]{1,0:T(8,128)(2,1)}, f32[768,768]{1,0:T(8,128)}, bf16[768,768]{1,0:T(8,128)(2,1)}, bf16[768,1920]{1,0:T(8,128)(2,1)}, bf16[768,1920]{1...) custom-call(s32[8,16]{1,0:T(8,128)} %stack.37.tab, ...), custom_call_target="tpu_custom_call" | custom-call | flops 24461180928 | bytes 34000000 | tf_op jit(solution)/shard_map/middle/pallas_call | solution.py:673
  246.1 37.6 %attention_back.1 = (bf16[768,768]{1,0:T(8,128)(2,1)}, bf16[3072,768]{1,0:T(8,128)(2,1)}, bf16[3072,768]{1,0:T(8,128)(2,1)}) custom-call(s32[64]{0:T(128)} %reshape.101.starts, bf16[768,768]{1,0:T(8,128)(2,1)} %get-tuple-element.39.q, bf16[3072,768]{1,0:T(8,128)(2,1)} %get-tuple-element.40.k, bf16[3072,768]{1,0:T(8,128)(2,1)} %get-tuple-element.41.v, ...), custom_call_target="tpu_custom_call" | custom-call | flops 20000000000 | bytes 24000000 | tf_op jit(solution)/shard_map/attention_back/pallas_call | solution.py:432
  283.7 19.3 %qkv_weight.1 = (bf16[768,1152]{1,0:T(8,128)(2,1)}, bf16[768,1152]{1,0:T(8,128)(2,1)}) custom-call(s32[8,16]{1,0:T(8,128)} %stack.37.tab, bf16[3072,768]{1,0:T(8,128)(2,1)} %get-tuple-element.55.normed, bf16[768,768]{1,0:T(8,128)(2,1)} %get-tuple-element.47.dq, bf16[3072,768]{1,0:T(8,128)(2,1)} %get-tuple-element.48.dk, bf16[3072,768]{1,0:T(8,128)(2,1)} %get-tuple-element.49.dv), custom_call_target="tpu_custom_call" | custom-call | flops 8153726976 | bytes 20000000 | tf_op jit(solution)/shard_map/qkv_weight/pallas_call | solution.py:793
  304.5 26.6 %qkv_back.1 = (bf16[3072,768]{1,0:T(8,128)(2,1)}, bf16[2,768,128]{2,1,0:T(8,128)(2,1)}) custom-call(s32[8,16]{1,0:T(8,128)} %stack.37.tab, bf16[768,768]{1,0:T(8,128)(2,1)} %bitcast.8.t0, bf16[768,768]{1,0:T(8,128)(2,1)} %collective-permute-done.t1, bf16[768,768]{1,0:T(8,128)(2,1)} %copy-done.14, bf16[768,768]{1,0:T(8,128)(2,1)} %collective-permute-done.2.t3, ...), custom_call_target="tpu_custom_call" | custom-call | flops 8153726976 | bytes 30000000 | tf_op jit(solution)/shard_map/qkv_back/pallas_call | solution.py:887
  331.0 0.9 slice_bitcast_fusion
  332.2 1.3 collective-permute-done.26
  333.5 1.0 fusion.2
  334.5 1.6 collective-permute-start.27
  336.1 3.1 collective-permute-done.27
  339.2 1.4 collective-permute-start.28
  341.0 1.7 collective-permute-start.33
  342.8 1.1 collective-permute-done.28
  343.8 65.6 %collective-permute-start.29 = (bf16[96,128]{1,0:T(8,128)(2,1)S(1)}, bf16[96,128]{1,0:T(8,128)(2,1)S(1)}, u32[]{:S(2)}, u32[]{:S(2)}) collective-permute-start(bf16[96,128]{1,0:T(8,128)(2,1)S(1)} %get-tuple-element.185), channel_id=1, source_target_pairs={{0,16},{1,17},{2,18},{3,19},{4,20},{5,21},{6,22},{7,23},{8,24},{9,... | collective-permute-start | bytes 73736 | tf_op jit(solution)/shard_map/ppermute | solution.py:958
  409.5 1.8 collective-permute-done.29
  411.3 4.0 collective-permute-start.30
  415.3 1.6 slice.369
  417.5 1.2 add_convert_fusion.13
  418.6 2.1 collective-permute-start.34
  423.0 4.3 collective-permute-done.34
  427.3 1.5 add_convert_fusion.19
  428.8 3.0 collective-permute-start.35
  431.8 2.9 add_convert_fusion.3
  434.7 2.1 collective-permute-start.45
  436.8 4.9 collective-permute-done.35
  442.5 1.6 add_convert_fusion.5
  444.9 1.7 collective-permute-done.36
  447.4 1.3 collective-permute-start.39
  448.9 7.7 %collective-permute-done.45 = bf16[1536,384]{1,0:T(8,128)(2,1)S(1)} collective-permute-done((bf16[1536,384]{1,0:T(8,128)(2,1)S(1)}, bf16[1536,384]{1,0:T(8,128)(2,1)S(1)}, u32[]{:S(2)}, u32[]{:S(2)}) %collective-permute-start.45) | collective-permute-done | bytes 1179680 | tf_op jit(solution)/shard_map/ppermute | solution.py:958
  457.7 48.5 %collective-permute-done.39 = bf16[384,1920]{1,0:T(8,128)(2,1)S(1)} collective-permute-done((bf16[384,1920]{1,0:T(8,128)(2,1)S(1)}, bf16[384,1920]{1,0:T(8,128)(2,1)S(1)}, u32[]{:S(2)}, u32[]{:S(2)}) %collective-permute-start.39) | collective-permute-done | bytes 1474592 | tf_op jit(solution)/shard_map/ppermute | solution.py:958
  506.7 2.1 collective-permute-start.40
  509.0 3.0 fusion
  512.0 7.7 %collective-permute-done.47 = bf16[384,384]{1,0:T(8,128)(2,1)S(1)} collective-permute-done((bf16[384,384]{1,0:T(8,128)(2,1)S(1)}, bf16[384,384]{1,0:T(8,128)(2,1)S(1)}, u32[]{:S(2)}, u32[]{:S(2)}) %collective-permute-start.47) | collective-permute-done | bytes 294944 | tf_op jit(solution)/shard_map/ppermute | solution.py:958
  520.1 2.5 collective-permute-start.41
  522.6 4.0 collective-permute-done.48
  526.8 5.9 %collective-permute-done.41 = bf16[96,1920]{1,0:T(8,128)(2,1)S(1)} collective-permute-done((bf16[96,1920]{1,0:T(8,128)(2,1)S(1)}, bf16[96,1920]{1,0:T(8,128)(2,1)S(1)}, u32[]{:S(2)}, u32[]{:S(2)}) %collective-permute-start.41) | collective-permute-done | bytes 368672 | tf_op jit(solution)/shard_map/ppermute | solution.py:958
  532.8 5.5 %collective-permute-done.42 = bf16[48,1920]{1,0:T(8,128)(2,1)S(1)} collective-permute-done((bf16[48,1920]{1,0:T(8,128)(2,1)S(1)}, bf16[48,1920]{1,0:T(8,128)(2,1)S(1)}, u32[]{:S(2)}, u32[]{:S(2)}) %collective-permute-start.42) | collective-permute-done | bytes 184352 | tf_op jit(solution)/shard_map/ppermute | solution.py:958
  (206 shorter events, 40.1 us)
Async XLA Ops:
  0.6 16.6 %copy-start.4 = (bf16[96,768]{1,0:T(8,128)(2,1)S(1)}, bf16[96,768]{1,0:T(8,128)(2,1)}, u32[]{:S(2)}) copy-start(bf16[96,768]{1,0:T(8,128)(2,1)} %param.35) | copy-start | bytes 442372
  1.7 15.6 %collective-permute-start.18 = (bf16[96,384]{1,0:T(8,128)(2,1)S(1)}, bf16[96,384]{1,0:T(8,128)(2,1)S(1)}, u32[]{:S(2)}, u32[]{:S(2)}) collective-permute-start(bf16[96,384]{1,0:T(8,128)(2,1)S(1)} %broadcast_select_fusion.6), channel_id=1, source_target_pairs={{0,1},{1,0},{2,3},{3,2},{4,5},{5,4},{6,7},{7,6},{8,9},{9,8},{10,11... | collective-permute-start | bytes 221192 | tf_op jit(solution)/shard_map/ppermute | solution.py:958
  10.9 2.4 collective-permute-start.6
  12.7 6.0 %collective-permute-start.12 = (bf16[24,1920]{1,0:T(8,128)(2,1)S(1)}, bf16[24,1920]{1,0:T(8,128)(2,1)S(1)}, u32[]{:S(2)}, u32[]{:S(2)}) collective-permute-start(bf16[24,1920]{1,0:T(8,128)(2,1)S(1)} %broadcast_select_fusion.2), channel_id=1, source_target_pairs={{0,1},{1,0},{2,3},{3,2},{4,5},{5,4},{6,7},{7,6},{8,9},{9,8},{10,11... | collective-permute-start | bytes 276488 | tf_op jit(solution)/shard_map/ppermute | solution.py:958
  13.9 8.2 %collective-permute-start.7 = (bf16[48,1280]{1,0:T(8,128)(2,1)S(1)}, bf16[48,1280]{1,0:T(8,128)(2,1)S(1)}, u32[]{:S(2)}, u32[]{:S(2)}) collective-permute-start(bf16[48,1280]{1,0:T(8,128)(2,1)S(1)} %pad_maximum_fusion.10), channel_id=1, source_target_pairs={{0,8},{1,9},{2,10},{3,11},{4,12},{5,13},{6,14},{7,15},{8,0},{9,1},... | collective-permute-start | bytes 368648 | tf_op jit(solution)/shard_map/ppermute | solution.py:958
  18.6 6.9 %collective-permute-start.19 = (bf16[192,384]{1,0:T(8,128)(2,1)S(1)}, bf16[192,384]{1,0:T(8,128)(2,1)S(1)}, u32[]{:S(2)}, u32[]{:S(2)}) collective-permute-start(bf16[192,384]{1,0:T(8,128)(2,1)S(1)} %pad_maximum_fusion.9), channel_id=1, source_target_pairs={{0,8},{1,9},{2,10},{3,11},{4,12},{5,13},{6,14},{7,15},{8,0},{9,1},... | collective-permute-start | bytes 442376 | tf_op jit(solution)/shard_map/ppermute | solution.py:958
  20.0 13.8 %collective-permute-start.13 = (bf16[48,1920]{1,0:T(8,128)(2,1)S(1)}, bf16[48,1920]{1,0:T(8,128)(2,1)S(1)}, u32[]{:S(2)}, u32[]{:S(2)}) collective-permute-start(bf16[48,1920]{1,0:T(8,128)(2,1)S(1)} %pad_maximum_fusion.8), channel_id=1, source_target_pairs={{0,8},{1,9},{2,10},{3,11},{4,12},{5,13},{6,14},{7,15},{8,0},{9,1},... | collective-permute-start | bytes 552968 | tf_op jit(solution)/shard_map/ppermute | solution.py:958
  22.1 29.3 %collective-permute-start.8 = (bf16[96,1280]{1,0:T(8,128)(2,1)S(1)}, bf16[96,1280]{1,0:T(8,128)(2,1)S(1)}, u32[]{:S(2)}, u32[]{:S(2)}) collective-permute-start(bf16[96,1280]{1,0:T(8,128)(2,1)S(1)} %pad_maximum_fusion.7), channel_id=1, source_target_pairs={{0,16},{1,17},{2,18},{3,19},{4,20},{5,21},{6,22},{7,23},{8,24},{9,... | collective-permute-start | bytes 737288 | tf_op jit(solution)/shard_map/ppermute | solution.py:958
  25.5 60.5 %collective-permute-start.20 = (bf16[384,384]{1,0:T(8,128)(2,1)S(1)}, bf16[384,384]{1,0:T(8,128)(2,1)S(1)}, u32[]{:S(2)}, u32[]{:S(2)}) collective-permute-start(bf16[384,384]{1,0:T(8,128)(2,1)S(1)} %pad_maximum_fusion.4), channel_id=1, source_target_pairs={{0,16},{1,17},{2,18},{3,19},{4,20},{5,21},{6,22},{7,23},{8,24},{9,... | collective-permute-start | bytes 884744 | tf_op jit(solution)/shard_map/ppermute | solution.py:958
  33.8 30.5 %collective-permute-start.14 = (bf16[96,1920]{1,0:T(8,128)(2,1)S(1)}, bf16[96,1920]{1,0:T(8,128)(2,1)S(1)}, u32[]{:S(2)}, u32[]{:S(2)}) collective-permute-start(bf16[96,1920]{1,0:T(8,128)(2,1)S(1)} %pad_maximum_fusion.3), channel_id=1, source_target_pairs={{0,16},{1,17},{2,18},{3,19},{4,20},{5,21},{6,22},{7,23},{8,24},{9,... | collective-permute-start | bytes 1105928 | tf_op jit(solution)/shard_map/ppermute | solution.py:958
  51.5 16.0 %collective-permute-start.9 = (bf16[192,1280]{1,0:T(8,128)(2,1)S(1)}, bf16[192,1280]{1,0:T(8,128)(2,1)S(1)}, u32[]{:S(2)}, u32[]{:S(2)}) collective-permute-start(bf16[192,1280]{1,0:T(8,128)(2,1)S(1)} %pad_maximum_fusion.2), channel_id=1, source_target_pairs={{0,4},{1,3},{2,6},{3,1},{4,0},{5,7},{6,2},{7,5},{8,12},{9,11},{10,... | collective-permute-start | bytes 1474568 | tf_op jit(solution)/shard_map/ppermute | solution.py:958
  64.4 17.9 %collective-permute-start.15 = (bf16[192,1920]{1,0:T(8,128)(2,1)S(1)}, bf16[192,1920]{1,0:T(8,128)(2,1)S(1)}, u32[]{:S(2)}, u32[]{:S(2)}) collective-permute-start(bf16[192,1920]{1,0:T(8,128)(2,1)S(1)} %pad_maximum_fusion), channel_id=1, source_target_pairs={{0,4},{1,3},{2,6},{3,1},{4,0},{5,7},{6,2},{7,5},{8,12},{9,11},{10,... | collective-permute-start | bytes 2211848 | tf_op jit(solution)/shard_map/ppermute | solution.py:958
  68.4 34.9 %collective-permute-start.10 = (bf16[384,1280]{1,0:T(8,128)(2,1)S(1)}, bf16[384,1280]{1,0:T(8,128)(2,1)S(1)}, u32[]{:S(2)}, u32[]{:S(2)}) collective-permute-start(bf16[384,1280]{1,0:T(8,128)(2,1)S(1)} %get-tuple-element.154), channel_id=1, source_target_pairs={{0,2},{1,5},{2,0},{3,7},{4,6},{5,1},{6,4},{7,3},{8,10},{9,13},{10,... | collective-permute-start | bytes 2949128 | tf_op jit(solution)/shard_map/ppermute | solution.py:958
  83.3 20.0 %copy-start.10 = (bf16[768,1920]{1,0:T(8,128)(2,1)}, bf16[768,1920]{1,0:T(8,128)(2,1)S(1)}, u32[]{:S(2)}) copy-start(bf16[768,1920]{1,0:T(8,128)(2,1)S(1)} %get-tuple-element.149) | copy-start | bytes 8847364
  83.3 35.8 %collective-permute-start.16 = (bf16[384,1920]{1,0:T(8,128)(2,1)}, bf16[384,1920]{1,0:T(8,128)(2,1)S(1)}, u32[]{:S(2)}, u32[]{:S(2)}) collective-permute-start(bf16[384,1920]{1,0:T(8,128)(2,1)} %get-tuple-element.148), channel_id=1, source_target_pairs={{0,2},{1,5},{2,0},{3,7},{4,6},{5,1},{6,4},{7,3},{8,10},{9,13},{10,... | collective-permute-start | bytes 4423688 | tf_op jit(solution)/shard_map/ppermute | solution.py:958
  86.0 16.3 %collective-permute-start.21 = (bf16[768,384]{1,0:T(8,128)(2,1)S(1)}, bf16[768,384]{1,0:T(8,128)(2,1)S(1)}, u32[]{:S(2)}, u32[]{:S(2)}) collective-permute-start(bf16[768,384]{1,0:T(8,128)(2,1)S(1)} %pad_maximum_fusion.1), channel_id=1, source_target_pairs={{0,4},{1,3},{2,6},{3,1},{4,0},{5,7},{6,2},{7,5},{8,12},{9,11},{10,... | collective-permute-start | bytes 1769480 | tf_op jit(solution)/shard_map/ppermute | solution.py:958
  87.6 56.8 %collective-permute-start = (bf16[768,768]{1,0:T(8,128)(2,1)}, bf16[768,768]{1,0:T(8,128)(2,1)}, u32[]{:S(2)}, u32[]{:S(2)}) collective-permute-start(bf16[768,768]{1,0:T(8,128)(2,1)} %bitcast.8.t0), channel_id=1, source_target_pairs={{0,2},{1,3},{2,0},{3,1},{4,6},{5,7},{6,4},{7,5},{8,10},{9,11},{10,... | collective-permute-start | bytes 3538952 | tf_op jit(solution)/shard_map/ppermute | solution.py:958
  103.3 43.1 %collective-permute-start.22 = (bf16[1536,384]{1,0:T(8,128)(2,1)}, bf16[1536,384]{1,0:T(8,128)(2,1)S(1)}, u32[]{:S(2)}, u32[]{:S(2)}) collective-permute-start(bf16[1536,384]{1,0:T(8,128)(2,1)} %get-tuple-element.152), channel_id=1, source_target_pairs={{0,2},{1,5},{2,0},{3,7},{4,6},{5,1},{6,4},{7,3},{8,10},{9,13},{10,... | collective-permute-start | bytes 3538952 | tf_op jit(solution)/shard_map/ppermute | solution.py:958
  105.0 40.6 %copy-start.7 = (s32[1,3072]{1,0:T(1,128)S(1)}, s32[1,3072]{1,0:T(1,128)}, u32[]{:S(2)}) copy-start(s32[1,3072]{1,0:T(1,128)} %param.22) | copy-start | bytes 36868
  105.0 46.3 %collective-permute-start.11 = (bf16[768,1280]{1,0:T(8,128)(2,1)}, bf16[768,1280]{1,0:T(8,128)(2,1)}, u32[]{:S(2)}, u32[]{:S(2)}) collective-permute-start(bf16[768,1280]{1,0:T(8,128)(2,1)} %constant_dynamic-update-slice_fusion.5.own), channel_id=1, source_target_pairs={{0,1},{1,0},{2,3},{3,2},{4,5},{5,4},{6,7},{7,6},{8,9},{9,8},{10,11... | collective-permute-start | bytes 5898248 | tf_op jit(solution)/shard_map/ppermute | solution.py:958
  105.0 39.4 %collective-permute-start.3 = (s32[1,768]{1,0:T(1,128)S(1)}, s32[1,768]{1,0:T(1,128)S(1)}, u32[]{:S(2)}, u32[]{:S(2)}) collective-permute-start(s32[1,768]{1,0:T(1,128)S(1)} %copy-done.9), channel_id=1, source_target_pairs={{0,2},{1,3},{2,0},{3,1},{4,6},{5,7},{6,4},{7,5},{8,10},{9,11},{10,... | collective-permute-start | bytes 9224 | tf_op jit(solution)/shard_map/ppermute | solution.py:958
  119.1 25.8 %collective-permute-start.4 = (s32[1,768]{1,0:T(1,128)S(1)}, s32[1,768]{1,0:T(1,128)S(1)}, u32[]{:S(2)}, u32[]{:S(2)}) collective-permute-start(s32[1,768]{1,0:T(1,128)S(1)} %copy-done.9), channel_id=1, source_target_pairs={{0,1},{1,0},{2,3},{3,2},{4,5},{5,4},{6,7},{7,6},{8,9},{9,8},{10,11... | collective-permute-start | bytes 9224 | tf_op jit(solution)/shard_map/ppermute | solution.py:958
  120.4 29.6 %copy-start.12 = (s32[16]{0:T(128)S(1)}, s32[16]{0:T(128)}, u32[]{:S(2)}) copy-start(s32[16]{0:T(128)} %constant.48.clone) | copy-start | bytes 196
  120.4 29.6 %copy-start.13 = (s32[16]{0:T(128)S(1)}, s32[16]{0:T(128)}, u32[]{:S(2)}) copy-start(s32[16]{0:T(128)} %constant.49.clone) | copy-start | bytes 196
  144.4 6.9 %collective-permute-start.1 = (bf16[768,768]{1,0:T(8,128)(2,1)}, bf16[768,768]{1,0:T(8,128)(2,1)S(1)}, u32[]{:S(2)}, u32[]{:S(2)}) collective-permute-start(bf16[768,768]{1,0:T(8,128)(2,1)} %bitcast.8.t0), channel_id=1, source_target_pairs={{0,1},{1,0},{2,3},{3,2},{4,5},{5,4},{6,7},{7,6},{8,9},{9,8},{10,11... | collective-permute-start | bytes 3538952 | tf_op jit(solution)/shard_map/ppermute | solution.py:958
  144.4 6.9 %collective-permute-start.2 = (bf16[768,768]{1,0:T(8,128)(2,1)}, bf16[768,768]{1,0:T(8,128)(2,1)}, u32[]{:S(2)}, u32[]{:S(2)}) collective-permute-start(bf16[768,768]{1,0:T(8,128)(2,1)} %collective-permute-done.t1), channel_id=1, source_target_pairs={{0,1},{1,0},{2,3},{3,2},{4,5},{5,4},{6,7},{7,6},{8,9},{9,8},{10,11... | collective-permute-start | bytes 3538952 | tf_op jit(solution)/shard_map/ppermute | solution.py:958
  144.9 54.7 %collective-permute-start.17 = (bf16[768,1920]{1,0:T(8,128)(2,1)}, bf16[768,1920]{1,0:T(8,128)(2,1)}, u32[]{:S(2)}, u32[]{:S(2)}) collective-permute-start(bf16[768,1920]{1,0:T(8,128)(2,1)} %constant_dynamic-update-slice_fusion.16.uo_own), channel_id=1, source_target_pairs={{0,1},{1,0},{2,3},{3,2},{4,5},{5,4},{6,7},{7,6},{8,9},{9,8},{10,11... | collective-permute-start | bytes 8847368 | tf_op jit(solution)/shard_map/ppermute | solution.py:958
  146.4 2.5 collective-permute-start.5
  148.9 50.7 %collective-permute-start.23 = (bf16[3072,384]{1,0:T(8,128)(2,1)}, bf16[3072,384]{1,0:T(8,128)(2,1)}, u32[]{:S(2)}, u32[]{:S(2)}) collective-permute-start(bf16[3072,384]{1,0:T(8,128)(2,1)} %constant_dynamic-update-slice_fusion.27.dn_own), channel_id=1, source_target_pairs={{0,1},{1,0},{2,3},{3,2},{4,5},{5,4},{6,7},{7,6},{8,9},{9,8},{10,11... | collective-permute-start | bytes 7077896 | tf_op jit(solution)/shard_map/ppermute | solution.py:958
  283.7 19.8 %copy-start.6 = (f32[4,768]{1,0:T(4,128)S(1)}, f32[4,768]{1,0:T(4,128)}, u32[]{:S(2)}) copy-start(f32[4,768]{1,0:T(4,128)} %get-tuple-element.52) | copy-start | bytes 36868
  283.7 20.0 %copy-start.5 = (f32[8,768]{1,0:T(8,128)S(1)}, f32[8,768]{1,0:T(8,128)}, u32[]{:S(2)}) copy-start(f32[8,768]{1,0:T(8,128)} %get-tuple-element.51) | copy-start | bytes 73732
  303.1 37.5 %collective-permute-start.32 = (bf16[768,1152]{1,0:T(8,128)(2,1)}, bf16[768,1152]{1,0:T(8,128)(2,1)S(1)}, u32[]{:S(2)}, u32[]{:S(2)}) collective-permute-start(bf16[768,1152]{1,0:T(8,128)(2,1)} %get-tuple-element.57), channel_id=1, source_target_pairs={{0,1},{1,0},{2,3},{3,2},{4,5},{5,4},{6,7},{7,6},{8,9},{9,8},{10,11... | collective-permute-start | bytes 5308424 | tf_op jit(solution)/shard_map/ppermute | solution.py:958
  304.5 36.1 %copy-start.3 = (bf16[768,1152]{1,0:T(8,128)(2,1)S(1)}, bf16[768,1152]{1,0:T(8,128)(2,1)}, u32[]{:S(2)}) copy-start(bf16[768,1152]{1,0:T(8,128)(2,1)} %get-tuple-element.56) | copy-start | bytes 5308420
  332.0 1.5 collective-permute-start.26
  334.5 4.7 collective-permute-start.27
  336.1 95.7 %collective-permute-start.44 = (bf16[3072,384]{1,0:T(8,128)(2,1)}, bf16[3072,384]{1,0:T(8,128)(2,1)}, u32[]{:S(2)}, u32[]{:S(2)}) collective-permute-start(bf16[3072,384]{1,0:T(8,128)(2,1)} %get-tuple-element.61), channel_id=1, source_target_pairs={{0,1},{1,0},{2,3},{3,2},{4,5},{5,4},{6,7},{7,6},{8,9},{9,8},{10,11... | collective-permute-start | bytes 7077896 | tf_op jit(solution)/shard_map/ppermute | solution.py:958
  339.2 4.6 collective-permute-start.28
  340.6 74.6 %copy-start = (bf16[3072,768]{1,0:T(8,128)(2,1)S(1)}, bf16[3072,768]{1,0:T(8,128)(2,1)}, u32[]{:S(2)}) copy-start(bf16[3072,768]{1,0:T(8,128)(2,1)} %get-tuple-element.53) | copy-start | bytes 14155780
  341.0 76.4 %collective-permute-start.33 = (bf16[384,1152]{1,0:T(8,128)(2,1)S(1)}, bf16[384,1152]{1,0:T(8,128)(2,1)S(1)}, u32[]{:S(2)}, u32[]{:S(2)}) collective-permute-start(bf16[384,1152]{1,0:T(8,128)(2,1)S(1)} %get-tuple-element.135), channel_id=1, source_target_pairs={{0,2},{1,5},{2,0},{3,7},{4,6},{5,1},{6,4},{7,3},{8,10},{9,13},{10,... | collective-permute-start | bytes 2654216 | tf_op jit(solution)/shard_map/ppermute | solution.py:958
  343.8 67.4 %collective-permute-start.29 = (bf16[96,128]{1,0:T(8,128)(2,1)S(1)}, bf16[96,128]{1,0:T(8,128)(2,1)S(1)}, u32[]{:S(2)}, u32[]{:S(2)}) collective-permute-start(bf16[96,128]{1,0:T(8,128)(2,1)S(1)} %get-tuple-element.185), channel_id=1, source_target_pairs={{0,16},{1,17},{2,18},{3,19},{4,20},{5,21},{6,22},{7,23},{8,24},{9,... | collective-permute-start | bytes 73736 | tf_op jit(solution)/shard_map/ppermute | solution.py:958
  411.3 6.1 %collective-permute-start.30 = (bf16[48,128]{1,0:T(8,128)(2,1)S(1)}, bf16[48,128]{1,0:T(8,128)(2,1)S(1)}, u32[]{:S(2)}, u32[]{:S(2)}) collective-permute-start(bf16[48,128]{1,0:T(8,128)(2,1)S(1)} %add_convert_fusion.30), channel_id=1, source_target_pairs={{0,8},{1,9},{2,10},{3,11},{4,12},{5,13},{6,14},{7,15},{8,0},{9,1},... | collective-permute-start | bytes 36872 | tf_op jit(solution)/shard_map/ppermute | solution.py:958
  415.2 31.5 %collective-permute-start.38 = (bf16[768,1920]{1,0:T(8,128)(2,1)}, bf16[768,1920]{1,0:T(8,128)(2,1)S(1)}, u32[]{:S(2)}, u32[]{:S(2)}) collective-permute-start(bf16[768,1920]{1,0:T(8,128)(2,1)} %get-tuple-element.59), channel_id=1, source_target_pairs={{0,1},{1,0},{2,3},{3,2},{4,5},{5,4},{6,7},{7,6},{8,9},{9,8},{10,11... | collective-permute-start | bytes 8847368 | tf_op jit(solution)/shard_map/ppermute | solution.py:958
  415.2 27.3 %slice-start = ((s8[4718592]{0:T(1024)(128)(4,1)}), s8[524288]{0:T(1024)(128)(4,1)S(1)}, s32[]{:S(2)}) async-start(s8[4718592]{0:T(1024)(128)(4,1)} %bitcast.34), calls=%async_computation | async-start | bytes 1048576
  416.8 25.7 %collective-permute-start.24 = (bf16[1536,768]{1,0:T(8,128)(2,1)}, bf16[1536,768]{1,0:T(8,128)(2,1)}, u32[]{:S(2)}, u32[]{:S(2)}) collective-permute-start(bf16[1536,768]{1,0:T(8,128)(2,1)} %slice.369), channel_id=1, source_target_pairs={{0,1},{1,0},{2,3},{3,2},{4,5},{5,4},{6,7},{7,6},{8,9},{9,8},{10,11... | collective-permute-start | bytes 7077896 | tf_op jit(solution)/shard_map/ppermute | solution.py:958
  417.4 3.3 collective-permute-start.31
  418.6 8.7 %collective-permute-start.34 = (bf16[192,1152]{1,0:T(8,128)(2,1)}, bf16[192,1152]{1,0:T(8,128)(2,1)}, u32[]{:S(2)}, u32[]{:S(2)}) collective-permute-start(bf16[192,1152]{1,0:T(8,128)(2,1)} %get-tuple-element.141), channel_id=1, source_target_pairs={{0,4},{1,3},{2,6},{3,1},{4,0},{5,7},{6,2},{7,5},{8,12},{9,11},{10,... | collective-permute-start | bytes 1327112 | tf_op jit(solution)/shard_map/ppermute | solution.py:958
  427.3 15.3 %slice-start.1 = ((s8[4718592]{0:T(1024)(128)(4,1)}), s8[4194304]{0:T(1024)(128)(4,1)S(1)}, s32[]{:S(2)}) async-start(s8[4718592]{0:T(1024)(128)(4,1)} %bitcast.34), calls=%async_computation.1 | async-start | bytes 8388608
  428.8 12.9 %collective-permute-start.35 = (bf16[96,1152]{1,0:T(8,128)(2,1)S(1)}, bf16[96,1152]{1,0:T(8,128)(2,1)S(1)}, u32[]{:S(2)}, u32[]{:S(2)}) collective-permute-start(bf16[96,1152]{1,0:T(8,128)(2,1)S(1)} %get-tuple-element.147), channel_id=1, source_target_pairs={{0,16},{1,17},{2,18},{3,19},{4,20},{5,21},{6,22},{7,23},{8,24},{9,... | collective-permute-start | bytes 663560 | tf_op jit(solution)/shard_map/ppermute | solution.py:958
  434.7 21.9 %collective-permute-start.45 = (bf16[1536,384]{1,0:T(8,128)(2,1)S(1)}, bf16[1536,384]{1,0:T(8,128)(2,1)S(1)}, u32[]{:S(2)}, u32[]{:S(2)}) collective-permute-start(bf16[1536,384]{1,0:T(8,128)(2,1)S(1)} %get-tuple-element.133), channel_id=1, source_target_pairs={{0,2},{1,5},{2,0},{3,7},{4,6},{5,1},{6,4},{7,3},{8,10},{9,13},{10,... | collective-permute-start | bytes 3538952 | tf_op jit(solution)/shard_map/ppermute | solution.py:958
  441.7 5.0 copy-start.1
  441.7 4.8 collective-permute-start.36
  444.2 64.9 %collective-permute-start.25 = (bf16[768,768]{1,0:T(8,128)(2,1)S(1)}, bf16[768,768]{1,0:T(8,128)(2,1)S(1)}, u32[]{:S(2)}, u32[]{:S(2)}) collective-permute-start(bf16[768,768]{1,0:T(8,128)(2,1)S(1)} %add_convert_fusion.5), channel_id=1, source_target_pairs={{0,2},{1,3},{2,0},{3,1},{4,6},{5,7},{6,4},{7,5},{8,10},{9,11},{10,... | collective-permute-start | bytes 3538952 | tf_op jit(solution)/shard_map/ppermute | solution.py:958
  446.6 2.2 collective-permute-start.37
  447.4 58.8 %collective-permute-start.39 = (bf16[384,1920]{1,0:T(8,128)(2,1)S(1)}, bf16[384,1920]{1,0:T(8,128)(2,1)S(1)}, u32[]{:S(2)}, u32[]{:S(2)}) collective-permute-start(bf16[384,1920]{1,0:T(8,128)(2,1)S(1)} %get-tuple-element.131), channel_id=1, source_target_pairs={{0,2},{1,5},{2,0},{3,7},{4,6},{5,1},{6,4},{7,3},{8,10},{9,13},{10,... | collective-permute-start | bytes 4423688 | tf_op jit(solution)/shard_map/ppermute | solution.py:958
  456.9 51.8 %collective-permute-start.46 = (bf16[768,384]{1,0:T(8,128)(2,1)S(1)}, bf16[768,384]{1,0:T(8,128)(2,1)S(1)}, u32[]{:S(2)}, u32[]{:S(2)}) collective-permute-start(bf16[768,384]{1,0:T(8,128)(2,1)S(1)} %get-tuple-element.139), channel_id=1, source_target_pairs={{0,4},{1,3},{2,6},{3,1},{4,0},{5,7},{6,2},{7,5},{8,12},{9,11},{10,... | collective-permute-start | bytes 1769480 | tf_op jit(solution)/shard_map/ppermute | solution.py:958
  457.7 48.9 %copy-start.8 = (f32[24,2304]{1,0:T(8,128)}, f32[24,2304]{1,0:T(8,128)S(1)}, u32[]{:S(2)}) copy-start(f32[24,2304]{1,0:T(8,128)S(1)} %constant_dynamic-update-slice_fusion.33) | copy-start | bytes 663556
  506.2 2.8 copy-start.2
  506.7 13.2 %collective-permute-start.40 = (bf16[192,1920]{1,0:T(8,128)(2,1)S(1)}, bf16[192,1920]{1,0:T(8,128)(2,1)S(1)}, u32[]{:S(2)}, u32[]{:S(2)}) collective-permute-start(bf16[192,1920]{1,0:T(8,128)(2,1)S(1)} %get-tuple-element.137), channel_id=1, source_target_pairs={{0,4},{1,3},{2,6},{3,1},{4,0},{5,7},{6,2},{7,5},{8,12},{9,11},{10,... | collective-permute-start | bytes 2211848 | tf_op jit(solution)/shard_map/ppermute | solution.py:958
  508.9 10.8 %collective-permute-start.47 = (bf16[384,384]{1,0:T(8,128)(2,1)S(1)}, bf16[384,384]{1,0:T(8,128)(2,1)S(1)}, u32[]{:S(2)}, u32[]{:S(2)}) collective-permute-start(bf16[384,384]{1,0:T(8,128)(2,1)S(1)} %get-tuple-element.145), channel_id=1, source_target_pairs={{0,16},{1,17},{2,18},{3,19},{4,20},{5,21},{6,22},{7,23},{8,24},{9,... | collective-permute-start | bytes 884744 | tf_op jit(solution)/shard_map/ppermute | solution.py:958
  519.8 6.8 %collective-permute-start.48 = (bf16[192,384]{1,0:T(8,128)(2,1)S(1)}, bf16[192,384]{1,0:T(8,128)(2,1)S(1)}, u32[]{:S(2)}, u32[]{:S(2)}) collective-permute-start(bf16[192,384]{1,0:T(8,128)(2,1)S(1)} %add_convert_fusion.22), channel_id=1, source_target_pairs={{0,8},{1,9},{2,10},{3,11},{4,12},{5,13},{6,14},{7,15},{8,0},{9,1},... | collective-permute-start | bytes 442376 | tf_op jit(solution)/shard_map/ppermute | solution.py:958
  520.1 12.6 %collective-permute-start.41 = (bf16[96,1920]{1,0:T(8,128)(2,1)S(1)}, bf16[96,1920]{1,0:T(8,128)(2,1)S(1)}, u32[]{:S(2)}, u32[]{:S(2)}) collective-permute-start(bf16[96,1920]{1,0:T(8,128)(2,1)S(1)} %get-tuple-element.143), channel_id=1, source_target_pairs={{0,16},{1,17},{2,18},{3,19},{4,20},{5,21},{6,22},{7,23},{8,24},{9,... | collective-permute-start | bytes 1105928 | tf_op jit(solution)/shard_map/ppermute | solution.py:958
  526.7 6.1 %collective-permute-start.49 = (bf16[96,384]{1,0:T(8,128)(2,1)S(1)}, bf16[96,384]{1,0:T(8,128)(2,1)S(1)}, u32[]{:S(2)}, u32[]{:S(2)}) collective-permute-start(bf16[96,384]{1,0:T(8,128)(2,1)S(1)} %select_convert_fusion.1), channel_id=1, source_target_pairs={{0,1},{1,0},{2,3},{3,2},{4,5},{5,4},{6,7},{7,6},{8,9},{9,8},{10,11... | collective-permute-start | bytes 221192 | tf_op jit(solution)/shard_map/ppermute | solution.py:958
  532.7 5.6 %collective-permute-start.42 = (bf16[48,1920]{1,0:T(8,128)(2,1)S(1)}, bf16[48,1920]{1,0:T(8,128)(2,1)S(1)}, u32[]{:S(2)}, u32[]{:S(2)}) collective-permute-start(bf16[48,1920]{1,0:T(8,128)(2,1)S(1)} %add_convert_fusion.20), channel_id=1, source_target_pairs={{0,8},{1,9},{2,10},{3,11},{4,12},{5,13},{6,14},{7,15},{8,0},{9,1},... | collective-permute-start | bytes 552968 | tf_op jit(solution)/shard_map/ppermute | solution.py:958
  538.4 1.4 collective-permute-start.43
  (3 other events, 5.3 us)
